TPU v7x, 256 devices: a whole 4x4x8 slice. The times are simulated.
256 devices in a mesh: cell: 32 (over y, z), view: 8 (over x, core).
Axes of the slice: x: 4, y: 4, z: 8, core: 2. Of those that a mesh axis runs over, the one named last changes fastest.
Arguments:
- gaussians: float32 [53, 262144], P(None, ('cell', 'view'))
- moment_one: float32 [53, 262144], P(None, ('cell', 'view')), may hold values from -4 to 4
- moment_two: float32 [53, 262144], P(None, ('cell', 'view')), may hold values from 0.01 to 1
- cameras: float32 [2, 2, 4], replicated, as said below
- target: bfloat16 [512, 8, 3, 256], P('cell', 'view'), may hold values from 0 to 1
- gauss_ids: int32 [32, 512, 8, 16], P('cell', None, 'view'), may hold values from 0 to 8191, as said below
- tile_counts: int32 [32, 512, 8], P('cell', None, 'view'), may hold values from 1 to 16
- intersection_slots: int32 [32, 32, 8, 2], P(None, None, 'view'), may hold values from -1 to 15, as said below
- depth_order: int32 [512, 8, 32], P('cell', 'view'), may hold values from 0 to 31, as said below
Outputs:
- rendered: float32 [512, 8, 3, 256], P('cell', 'view')
- new_gaussians: float32 [53, 262144], P(None, ('cell', 'view'))
- new_moment_one: float32 [53, 262144], P(None, ('cell', 'view'))
- new_moment_two: float32 [53, 262144], P(None, ('cell', 'view'))
Inputs may be any that keep to these rules, and one draw needn't show every extreme that they name: `gauss_ids`: the live entries of a list are distinct and increasing; over all lists of a cell no Gaussian is named by two live slots; entries at slots at or after the list's count are not read. `intersection_slots`: each list holds a run of consecutive tile offsets within the owner's 16 tiles, followed by -1 for empty slots. `depth_order`: each row is a permutation of the cells. `cameras`: the cross product of the two camera rows' first three entries has a positive third component.
All inputs are finite; a program needn't handle non-finite values.
Results may differ from a plain program's by a relative error of at most 0.0003.
Values sent between devices are 32-bit elements; how exact they have to be, the bound alone decides.
A program may use at most 128 MiB of HBM per device.

v0:
```python
import jax
import jax.numpy as jnp
from jax import lax
from jax.sharding import PartitionSpec as P

TSIDE = 16
TROW = 32


band_zero = 0.28209479177387814
band_one = 0.4886025119029199
band_two = (
    1.0925484305920792,
    -1.0925484305920792,
    0.31539156525252005,
    -1.0925484305920792,
    0.5462742152960396,
)
band_three = (
    -0.5900435899266435,
    2.890611442640554,
    -0.4570457994644658,
    0.3731763325901154,
    -0.4570457994644658,
    1.445305721320277,
    -0.5900435899266435,
)
beta_one = 0.9
beta_two = 0.999
learn_rate = 0.01
adam_eps = 1e-08
adam_step = 10.0


def view_basis(camera):
    normal = jnp.cross(camera[0, :3], camera[1, :3])
    unit_dir = normal / jnp.sqrt(jnp.sum(normal * normal))
    comp_x, comp_y, comp_z = (unit_dir[0], unit_dir[1], unit_dir[2])
    sq_x, sq_y, sq_z = (comp_x * comp_x, comp_y * comp_y, comp_z * comp_z)
    sh_list = [
        comp_x * 0.0 + band_zero,
        -band_one * comp_y,
        band_one * comp_z,
        -band_one * comp_x,
        band_two[0] * comp_x * comp_y,
        band_two[1] * comp_y * comp_z,
        band_two[2] * (2.0 * sq_z - sq_x - sq_y),
        band_two[3] * comp_x * comp_z,
        band_two[4] * (sq_x - sq_y),
        band_three[0] * comp_y * (3.0 * sq_x - sq_y),
        band_three[1] * comp_x * comp_y * comp_z,
        band_three[2] * comp_y * (4.0 * sq_z - sq_x - sq_y),
        band_three[3] * comp_z * (2.0 * sq_z - 3.0 * sq_x - 3.0 * sq_y),
        band_three[4] * comp_x * (4.0 * sq_z - sq_x - sq_y),
        band_three[5] * comp_z * (sq_x - sq_y),
        band_three[6] * comp_x * (sq_x - 3.0 * sq_y),
    ]
    return jnp.stack(sh_list)


def live_mask(counts_rows, listed, length):
    slot_ids = jnp.arange(length, dtype=jnp.int32)
    return ((slot_ids[None, :] < counts_rows[:, None]) & listed[:, None]).astype(jnp.float32)


def render_tiles(
    cell_params,
    list_ids,
    counts_rows,
    listed,
    tile_rows,
    view_group,
    cameras,
    half_views,
    rows_total,
):
    camera = lax.dynamic_index_in_dim(cameras, view_group // half_views, 0, keepdims=False)
    picked = jnp.take(cell_params, list_ids, axis=1)
    screen_x = (
        camera[0, 0] * picked[0]
        + camera[0, 1] * picked[1]
        + camera[0, 2] * picked[2]
        + camera[0, 3]
    )
    screen_y = (
        camera[1, 0] * picked[0]
        + camera[1, 1] * picked[1]
        + camera[1, 2] * picked[2]
        + camera[1, 3]
    )
    inv_var = jnp.exp(-2.0 * picked[3])
    opacity = jax.nn.sigmoid(picked[4])
    coeffs = picked[5:].reshape(3, 16, list_ids.shape[0], list_ids.shape[1])
    sh_terms = view_basis(camera)
    colour = 0.5 + jnp.einsum("b,cbrk->crk", sh_terms, coeffs, precision=lax.Precision.HIGHEST)
    window_tile = view_group % half_views * rows_total + tile_rows
    anchor_x = (window_tile % TROW * TSIDE).astype(jnp.float32)
    anchor_y = (window_tile // TROW * TSIDE).astype(jnp.float32)
    pixel_ids = jnp.arange(TSIDE * TSIDE, dtype=jnp.int32)
    off_x = (pixel_ids % TSIDE).astype(jnp.float32) + 0.5
    off_y = (pixel_ids // TSIDE).astype(jnp.float32) + 0.5
    delta_x = anchor_x[:, None, None] + off_x[None, None, :] - screen_x[:, :, None]
    delta_y = anchor_y[:, None, None] + off_y[None, None, :] - screen_y[:, :, None]
    distance = delta_x * delta_x + delta_y * delta_y
    live_slots = live_mask(counts_rows, listed, list_ids.shape[1])
    opacity_px = (opacity * live_slots)[:, :, None] * jnp.exp(-0.5 * distance * inv_var[:, :, None])
    log_keep = jnp.log1p(-opacity_px)
    before = jnp.cumsum(log_keep, axis=1) - log_keep
    weight = opacity_px * jnp.exp(before)
    partial_value = jnp.einsum("crk,rkp->rcp", colour, weight, precision=lax.Precision.HIGHEST)
    through = jnp.exp(jnp.sum(log_keep, axis=1))
    return (partial_value, through, live_slots)


def merge_tiles(colour, through, tile_order):
    colour_t = jnp.transpose(colour, (1, 0, 2, 3))
    through_t = jnp.transpose(through, (1, 0, 2))
    colour_s = jnp.take_along_axis(colour_t, tile_order[:, :, None, None], axis=1)
    through_s = jnp.take_along_axis(through_t, tile_order[:, :, None], axis=1)
    ahead = jnp.cumprod(through_s, axis=1)
    prefix = jnp.concatenate([jnp.ones_like(ahead[:, :1]), ahead[:, :-1]], axis=1)
    return jnp.sum(prefix[:, :, None, :] * colour_s, axis=1)


def adam_update(params, gradient, first_moment, second, touched):
    new_first = beta_one * first_moment + (1.0 - beta_one) * gradient
    new_second = beta_two * second + (1.0 - beta_two) * gradient * gradient
    fix_one = 1.0 - beta_one**adam_step
    fix_two = 1.0 - beta_two**adam_step
    change = learn_rate * (new_first / fix_one) / (jnp.sqrt(new_second / fix_two) + adam_eps)
    touched_mask = touched > 0.5
    return (
        jnp.where(touched_mask, params - change, params),
        jnp.where(touched_mask, new_first, first_moment),
        jnp.where(touched_mask, new_second, second),
    )


def per_device(
    gaussians,
    moment_one,
    moment_two,
    cameras,
    target,
    gauss_ids,
    tile_counts,
    intersection_slots,
    depth_order,
):
    cell_index = lax.axis_index("cell")
    view_group = lax.axis_index("view")
    cell_count = lax.axis_size("cell")
    half_views = lax.axis_size("view") // 2
    own_tiles = depth_order.shape[0]
    rows_total = own_tiles * cell_count
    pixels = target.shape[3]
    cell_params = lax.all_gather(gaussians, "view", axis=1, tiled=True)
    local_ids = gauss_ids[0, :, 0, :]
    local_counts = tile_counts[0, :, 0]
    own_slots = lax.dynamic_index_in_dim(intersection_slots, cell_index, 0, keepdims=False)[:, 0, :]
    tile_order = depth_order[:, 0, :]
    offsets = jnp.arange(own_tiles, dtype=jnp.int32)
    tile_rows = jnp.arange(rows_total, dtype=jnp.int32)
    listed = jnp.any(own_slots[:, :, None] == offsets[None, None, :], axis=1).reshape(-1)

    def forward(params):
        partial_value, through, unused = render_tiles(
            params,
            local_ids,
            local_counts,
            listed,
            tile_rows,
            view_group,
            cameras,
            half_views,
            rows_total,
        )
        return (partial_value, through)

    (partial_value, through), pull_back = jax.vjp(forward, cell_params)

    def merge_fixed(colour_in, through_in):
        return merge_tiles(colour_in, through_in, tile_order)

    truth = target[:, 0].astype(jnp.float32)
    got_colour, got_through = (
        lax.all_to_all(partial_value, "cell", split_axis=0, concat_axis=0, tiled=True),
        lax.all_to_all(through, "cell", split_axis=0, concat_axis=0, tiled=True),
    )
    dense_colour = got_colour.reshape(cell_count, own_tiles, 3, pixels)
    dense_through = got_through.reshape(cell_count, own_tiles, pixels)
    rendered, merge_back = jax.vjp(merge_fixed, dense_colour, dense_through)
    grad_colour, grad_through = merge_back(rendered - truth)
    back_colour, back_through = (
        lax.all_to_all(
            grad_colour.reshape(rows_total, 3, pixels),
            "cell",
            split_axis=0,
            concat_axis=0,
            tiled=True,
        ),
        lax.all_to_all(
            grad_through.reshape(rows_total, pixels),
            "cell",
            split_axis=0,
            concat_axis=0,
            tiled=True,
        ),
    )
    gradient = pull_back((back_colour, back_through))[0]
    live_slots = live_mask(local_counts, listed, local_ids.shape[1])
    touch_count = (
        jnp.zeros((cell_params.shape[1],), jnp.float32)
        .at[local_ids.reshape(-1)]
        .add(live_slots.reshape(-1))
    )
    grad_part, touched = (
        lax.psum_scatter(gradient, "view", scatter_dimension=1, tiled=True),
        lax.psum_scatter(touch_count, "view", scatter_dimension=0, tiled=True),
    )
    new_gaussians, new_one, new_two = adam_update(
        gaussians, grad_part, moment_one, moment_two, touched
    )
    return (rendered[:, None], new_gaussians, new_one, new_two)


def solution(mesh):
    placed = (
        P(None, ("cell", "view")),
        P(None, ("cell", "view")),
        P(None, ("cell", "view")),
        P(),
        P("cell", "view", None, None),
        P("cell", None, "view", None),
        P("cell", None, "view"),
        P(None, None, "view", None),
        P("cell", "view", None),
    )
    return jax.shard_map(
        per_device,
        mesh=mesh,
        in_specs=placed,
        out_specs=(
            P("cell", "view", None, None),
            P(None, ("cell", "view")),
            P(None, ("cell", "view")),
            P(None, ("cell", "view")),
        ),
        check_vma=False,
    )
```

profile of v0, /device:TPU:32, one launch (start us, length us, event | category | flops | bytes accessed | tf_op | source)
XLA Modules:
  0.0 607.5 jit_solution(416400810384153844)
XLA Ops:
  7.2 2.0 copy.209
  39.2 1.0 broadcast_add_fusion.1
  40.2 7.0 %all-gather.2.cloned.1.call-done = f32[53,8192]{0,1:T(8,128)} async-done(((f32[53,1024]{0,1:T(8,128)}), f32[53,8192]{0,1:T(8,128)}) %all-gather.2.cloned.1.call-update) | async-done | bytes 1736720 | tf_op jit(solution)/shard_map/all_gather | solution.py:157
  47.2 30.1 %gather_fusion = f32[8192,53]{1,0:T(8,128)} fusion(f32[53,8192]{0,1:T(8,128)} %all-gather.2.cloned.1.call-done, s32[8192]{0:T(1024)S(1)} %broadcast_clamp_fusion), kind=kCustom, calls=%fused_computation | custom fusion | bytes 3506176 | tf_op jit(solution)/shard_map/jvp(jit(_take))/gather | solution.py:78
  77.3 3.5 copy.211
  81.4 1.7 fusion.33
  83.1 1.4 copy.246
  84.5 5.7 fusion.55
  90.7 9.7 %fusion.26 = (f32[512,16,256]{2,1,0:T(8,128)}, f32[512,256]{1,0:T(8,128)S(1)}) fusion(f32[512,16]{1,0:T(8,128)S(1)} %copy.215, f32[512,16]{1,0:T(8,128)S(1)} %copy.214, f32[512,256]{1,0:T(8,128)} %broadcast_add_fusion, f32[512,16]{1,0:T(8,128)S(1)} %copy.213, f32[512,256]{1,0:T(8,128)} %broadcast_add_fusion.1, f32[512,16]{1,0:T(8,128)S(1)} %copy.212), kind=kLoop, calls=%fused_computation.40 | loop fusion | flops 18743296 | bytes 10092544 | tf_op jit(solution)/shard_map/jvp()/log1p | solution.py:107
  100.6 11.7 %fusion.24 = f32[512,16,256]{2,0,1:T(8,128)} fusion(f32[512,16,256]{2,1,0:T(8,128)} %get-tuple-element.50), kind=kOutput, calls=%fused_computation.37 | output fusion | flops 31457280 | bytes 16777216 | tf_op jit(solution)/shard_map/jvp(jit(cumsum))/reduce_window_sum | solution.py:108
  113.2 20.9 %all-to-all-start = ((f32[32,16,256]{2,1,0:T(8,128)}), f32[32,16,256]{2,1,0:T(8,128)S(1)}, u32[]{:S(2)}, u32[]{:S(2)}) async-start(f32[32,16,256]{2,1,0:T(8,128)} %bitcast.142), calls=%async_computation | async-start | bytes 1048576 | tf_op jit(solution)/shard_map/all_to_all | solution.py:188
  134.1 19.5 %fusion.29 = f32[512,3,256]{2,1,0:T(4,128)} fusion(f32[512,16]{1,0:T(8,128)S(1)} %copy-done.22, f32[512,16]{1,0:T(8,128)S(1)} %copy.214, f32[512,256]{1,0:T(8,128)S(1)} %copy-done.4, f32[512,16]{1,0:T(8,128)S(1)} %copy.213, f32[512,256]{1,0:T(8,128)S(1)} %copy-done.6, f32[512,16]{1,0:T(8,128)S(1)} %copy-done.19, f32[1,3,512,16]{3,1,2,0:T(4,128)} %copy.246, ...), kind=kOutput, calls=%fused_computation.42 | convolution fusion | flops 96493568 | bytes 11239424 | tf_op jit(solution)/shard_map/jvp(crk,rkp->rcp)/dot_general | solution.py:110
  154.4 9.8 %all-to-all-start.1 = ((f32[512,3,256]{2,1,0:T(4,128)}), f32[512,3,256]{2,1,0:T(4,128)S(1)}, u32[]{:S(2)}, u32[]{:S(2)}) async-start(f32[512,3,256]{2,1,0:T(4,128)} %fusion.29), calls=%async_computation.1 | async-start | bytes 4194304 | tf_op jit(solution)/shard_map/all_to_all | solution.py:187
  164.4 1.4 copy.277
  165.7 6.4 %gather_fusion.1 = f32[512,256]{1,0:T(8,128)} fusion(f32[16,32,256]{2,1,0:T(8,128)S(1)} %bitcast.132, s32[512]{0:T(512)S(1)} %reshape.666), kind=kCustom, calls=%fused_computation.1 | custom fusion | bytes 1052672 | tf_op jit(solution)/shard_map/jvp(jit(take_along_axis))/gather | solution.py:119
  172.1 1.2 broadcast_select_fusion
  173.3 1.4 slice.233
  175.0 1.8 mul.618
  176.8 1.6 slice.236
  178.4 1.6 slice.237
  180.0 1.6 mul.619
  182.6 1.5 slice.240
  184.1 1.5 mul.620
  185.6 1.4 slice.242
  187.9 1.5 slice.249
  189.4 1.5 slice.284
  190.9 1.6 slice.251
  192.5 1.5 slice.283
  194.0 1.4 slice.253
  196.9 1.0 slice_multiply_fusion.11
  202.5 5.8 pad.338
  208.2 1.0 fusion.44
  210.0 5.8 pad.277
  215.8 1.3 slice_add_fusion.3
  217.9 1.3 copy-done.2
  219.2 4.5 gather_fusion.2
  223.7 1.8 multiply_reduce_fusion.1
  226.3 8.0 %multiply_reduce_fusion = (f32[16,32,256]{2,1,0:T(8,128)S(1)}, f32[16,32,3,256]{3,2,1,0:T(4,128)}) fusion(f32[16,32,3,256]{3,2,1,0:T(4,128)S(1)} %bitcast.133, f32[16,3,256]{2,1,0:T(4,128)S(1)} %convert_subtract_fusion, pred[16,32]{1,0:T(8,128)(4,1)S(1)} %compare_and_fusion.1, f32[16,32,256]{2,1,0:T(8,128)} %concatenate.27), kind=kLoop, calls=%fused_computation.43 | loop fusion | flops 1441792 | bytes 4243968 | tf_op jit(solution)/shard_map/transpose(jvp())/reduce_sum | solution.py:122
  234.8 1.8 slice_multiply_fusion.1
  237.2 1.1 slice_multiply_fusion.3
  245.7 26.9 %scatter_fusion.1 = f32[16,32,256]{2,1,0:T(8,128)S(1)} fusion(f32[16,32,256]{2,1,0:T(8,128)S(1)} %broadcast_in_dim.105, s32[512]{0:T(512)S(1)} %reshape.694, f32[512,256]{1,0:T(8,128)S(1)} %bitcast.143), kind=kCustom, calls=%fused_computation.6 | custom fusion | flops 131072 | bytes 1576960 | tf_op jit(solution)/shard_map/transpose(jvp(jit(take_along_axis)))/scatter-add | solution.py:119
  272.6 1.1 copy.226
  273.7 9.8 %all-to-all-start.3 = ((f32[32,16,256]{2,1,0:T(8,128)}), f32[32,16,256]{2,1,0:T(8,128)}, u32[]{:S(2)}, u32[]{:S(2)}) async-start(f32[32,16,256]{2,1,0:T(8,128)} %copy.226), calls=%async_computation.3 | async-start | bytes 1048576 | tf_op jit(solution)/shard_map/all_to_all | solution.py:202
  284.0 38.9 %scatter_fusion = f32[16,32,3,256]{3,2,1,0:T(4,128)S(1)} fusion(f32[16,32,3,256]{3,2,1,0:T(4,128)S(1)} %broadcast_in_dim.103, s32[512]{0:T(512)S(1)} %reshape.694, f32[512,3,256]{2,1,0:T(4,128)} %bitcast.135), kind=kCustom, calls=%fused_computation.5 | custom fusion | flops 393216 | bytes 4722688 | tf_op jit(solution)/shard_map/transpose(jvp(jit(take_along_axis)))/scatter-add | solution.py:118
  322.9 1.9 copy.224
  324.8 9.8 %all-to-all-start.2 = ((f32[512,3,256]{2,1,0:T(4,128)}), f32[512,3,256]{2,1,0:T(4,128)}, u32[]{:S(2)}, u32[]{:S(2)}) async-start(f32[512,3,256]{2,1,0:T(4,128)} %bitcast.137), calls=%async_computation.2 | async-start | bytes 4194304 | tf_op jit(solution)/shard_map/all_to_all | solution.py:195
  335.8 2.1 bitcast_multiply_fusion
  337.9 46.0 %all-to-all-done.2 = f32[512,3,256]{2,1,0:T(4,128)} async-done(((f32[512,3,256]{2,1,0:T(4,128)}), f32[512,3,256]{2,1,0:T(4,128)}, u32[]{:S(2)}, u32[]{:S(2)}) %all-to-all-start.2) | async-done | bytes 1572896 | tf_op jit(solution)/shard_map/all_to_all | solution.py:195
  383.9 22.1 %fusion.35 = f32[3,512,16]{2,0,1:T(4,128)} fusion(f32[512,3,256]{2,1,0:T(4,128)} %all-to-all-done.2, f32[512,16]{1,0:T(8,128)} %copy-done.21, f32[512,16]{1,0:T(8,128)} %copy-done.16, f32[512,256]{1,0:T(8,128)S(1)} %copy-done.4, f32[512,16]{1,0:T(8,128)S(1)} %copy-done.14, f32[512,256]{1,0:T(8,128)S(1)} %copy-done.7, f32[512,16]{1,0:T(8,128)} %copy-done.18, ...), kind=kOutput, calls=%fused_computation.51 | convolution fusion | flops 96468992 | bytes 11239424 | tf_op jit(solution)/shard_map/transpose(jvp(crk,rkp->rcp))/dot_general | solution.py:110
  406.0 1.5 copy.225
  407.7 20.9 %fusion.12 = (f32[512,16,256]{2,1,0:T(8,128)}, f32[512,16,256]{2,1,0:T(8,128)}) fusion(f32[512,16]{1,0:T(8,128)} %copy-done.21, f32[512,16]{1,0:T(8,128)S(1)} %copy-done.17, f32[512,256]{1,0:T(8,128)S(1)} %copy-done.5, f32[512,16]{1,0:T(8,128)S(1)} %copy-done.15, f32[512,256]{1,0:T(8,128)S(1)} %copy-done.8, f32[512,16]{1,0:T(8,128)} %copy-done.18, ...), kind=kOutput, calls=%fused_computation.23 | convolution fusion | flops 98590720 | bytes 28016640 | tf_op jit(solution)/shard_map/transpose(jvp(crk,rkp->rcp))/dot_general | solution.py:110
  428.7 8.4 %fusion.21 = f32[512,16,256]{2,0,1:T(8,128)S(1)} fusion(f32[512,16,256]{2,1,0:T(8,128)} %get-tuple-element.105), kind=kOutput, calls=%fused_computation.33 | output fusion | flops 31457280 | bytes 16777216 | tf_op jit(solution)/shard_map/transpose(jvp(jit(cumsum)))/reduce_window_sum | solution.py:108
  437.2 29.2 %fusion.17 = (f32[512,16]{1,0:T(8,128)}, f32[512,16]{1,0:T(8,128)}, f32[512,16]{1,0:T(8,128)}, f32[512,16]{1,0:T(8,128)}) fusion(f32[512,16]{1,0:T(8,128)S(1)} %copy-done.33, f32[512,16]{1,0:T(8,128)S(1)} %copy-done.17, f32[512,256]{1,0:T(8,128)S(1)} %copy-done.5, f32[512,16]{1,0:T(8,128)S(1)} %copy-done.23, f32[512,16]{1,0:T(8,128)S(1)} %copy-done.15, ...), kind=kLoop, calls=%fused_computation.28 | loop fusion | flops 71270400 | bytes 27033600 | tf_op jit(solution)/shard_map/transpose(jvp())/reduce_sum | solution.py:103
  466.4 1.0 copy.229
  467.4 1.1 copy.230
  468.5 1.1 copy.232
  469.5 2.0 multiply_bitcast_fusion.5
  471.5 1.0 copy.233
  472.6 1.8 multiply_bitcast_fusion.2
  475.5 4.1 copy.234
  479.6 46.5 %scatter_custom_fusion.1 = f32[53,8192]{0,1:T(8,128)} fusion(s32[8192]{0:T(1024)} %copy-done.44, f32[8192,53]{1,0:T(8,128)} %bitcast.140, f32[]{:T(128)} %constant.204.clone.1), kind=kCustom, calls=%fused_computation.44 | custom fusion | flops 434176 | bytes 1737216 | tf_op jit(solution)/shard_map/transpose(jvp(jit(_take)))/scatter-add | solution.py:78
  527.3 43.5 %scatter_custom_fusion = f32[8192]{0:T(1024)S(1)} fusion(s32[8192]{0:T(1024)S(1)} %bitcast.147, f32[8192]{0:T(1024)S(1)} %reshape.682, f32[]{:T(128)} %constant.204.clone.1), kind=kCustom, calls=%fused_computation.132 | custom fusion | flops 8192 | bytes 32772 | tf_op jit(solution)/shard_map/scatter-add | solution.py:215
  572.0 23.6 %all-reduce.43 = f32[8192]{0:T(1024)S(1)} all-reduce(f32[8192]{0:T(1024)S(1)} %scatter_custom_fusion), channel_id=2, replica_groups=mesh['cell'=32,'view'=8] {'view'}, use_global_device_ids=true, to_apply=%region_6.7.clone | all-reduce | flops 8192 | bytes 65536
  596.3 1.5 fusion.43
  (232 shorter events, 35.2 us)
Async XLA Ops:
  7.2 29.9 %copy-start = (s32[32,32,1,2]{1,3,2,0:T(2,128)S(1)}, s32[32,32,1,2]{1,3,2,0:T(2,128)}, u32[]{:S(2)}) copy-start(s32[32,32,1,2]{1,3,2,0:T(2,128)} %param.16) | copy-start | bytes 24580
  7.2 40.0 %all-gather.2.cloned.1.call-start = ((), (), s32[]{:S(2)}) async-start(), calls=%async_computation.5 | async-start | bytes 4718592 | tf_op jit(solution)/shard_map/all_gather | solution.py:157
  37.1 40.2 %copy-start.44 = (s32[8192]{0:T(1024)}, s32[8192]{0:T(1024)S(1)}, u32[]{:S(2)}) copy-start(s32[8192]{0:T(1024)S(1)} %reshape.660) | copy-start | bytes 98308
  37.3 53.1 %copy-start.48 = (pred[512]{0:T(512)(128)(4,1)}, pred[512]{0:T(512)(128)(4,1)S(1)}, u32[]{:S(2)}) copy-start(pred[512]{0:T(512)(128)(4,1)S(1)} %and.113) | copy-start | bytes 1540
  37.4 43.9 %copy-start.50 = (f32[16]{0:T(128)}, f32[16]{0:T(128)S(1)}, u32[]{:S(2)}) copy-start(f32[16]{0:T(128)S(1)} %stack.43) | copy-start | bytes 196
  77.3 13.1 %copy-start.46 = (s32[1,512,1]{1,2,0:T(1,128)S(1)}, s32[1,512,1]{1,2,0:T(1,128)}, u32[]{:S(2)}) copy-start(s32[1,512,1]{1,2,0:T(1,128)} %param.15) | copy-start | bytes 6148
  81.1 19.3 %copy-start.3 = (f32[53,512,16]{1,2,0:T(8,128)}, f32[53,512,16]{1,2,0:T(8,128)S(1)}, u32[]{:S(2)}) copy-start(f32[53,512,16]{1,2,0:T(8,128)S(1)} %select_bitcast_fusion) | copy-start | bytes 5210116
  90.2 43.8 %copy-start.13 = (f32[512,16]{1,0:T(8,128)}, f32[512,16]{1,0:T(8,128)S(1)}, u32[]{:S(2)}) copy-start(f32[512,16]{1,0:T(8,128)S(1)} %copy.213) | copy-start | bytes 98308
  90.4 43.7 %copy-start.16 = (f32[512,16]{1,0:T(8,128)}, f32[512,16]{1,0:T(8,128)S(1)}, u32[]{:S(2)}) copy-start(f32[512,16]{1,0:T(8,128)S(1)} %copy.214) | copy-start | bytes 98308
  90.6 9.9 %copy-start.18 = (f32[512,16]{1,0:T(8,128)}, f32[512,16]{1,0:T(8,128)S(1)}, u32[]{:S(2)}) copy-start(f32[512,16]{1,0:T(8,128)S(1)} %copy.212) | copy-start | bytes 98308
  90.7 9.8 %copy-start.21 = (f32[512,16]{1,0:T(8,128)}, f32[512,16]{1,0:T(8,128)S(1)}, u32[]{:S(2)}) copy-start(f32[512,16]{1,0:T(8,128)S(1)} %copy.215) | copy-start | bytes 98308
  100.5 11.8 %copy-start.10 = (f32[512,256]{1,0:T(8,128)}, f32[512,256]{1,0:T(8,128)S(1)}, u32[]{:S(2)}) copy-start(f32[512,256]{1,0:T(8,128)S(1)} %get-tuple-element.51) | copy-start | bytes 1572868
  100.5 33.5 %copy-start.4 = (f32[512,256]{1,0:T(8,128)S(1)}, f32[512,256]{1,0:T(8,128)}, u32[]{:S(2)}) copy-start(f32[512,256]{1,0:T(8,128)} %broadcast_add_fusion) | copy-start | bytes 1572868
  100.5 33.5 %copy-start.6 = (f32[512,256]{1,0:T(8,128)S(1)}, f32[512,256]{1,0:T(8,128)}, u32[]{:S(2)}) copy-start(f32[512,256]{1,0:T(8,128)} %broadcast_add_fusion.1) | copy-start | bytes 1572868
  100.5 33.5 %copy-start.19 = (f32[512,16]{1,0:T(8,128)S(1)}, f32[512,16]{1,0:T(8,128)}, u32[]{:S(2)}) copy-start(f32[512,16]{1,0:T(8,128)} %copy-done.18) | copy-start | bytes 98308
  100.5 33.5 %copy-start.22 = (f32[512,16]{1,0:T(8,128)S(1)}, f32[512,16]{1,0:T(8,128)}, u32[]{:S(2)}) copy-start(f32[512,16]{1,0:T(8,128)} %copy-done.21) | copy-start | bytes 98308
  113.2 40.4 %all-to-all-start = ((f32[32,16,256]{2,1,0:T(8,128)}), f32[32,16,256]{2,1,0:T(8,128)S(1)}, u32[]{:S(2)}, u32[]{:S(2)}) async-start(f32[32,16,256]{2,1,0:T(8,128)} %bitcast.142), calls=%async_computation | async-start | bytes 1048576 | tf_op jit(solution)/shard_map/all_to_all | solution.py:188
  134.1 30.1 %copy-start.45 = (s32[16,1,32]{2,1,0:T(1,128)S(1)}, s32[16,1,32]{2,1,0:T(1,128)}, u32[]{:S(2)}) copy-start(s32[16,1,32]{2,1,0:T(1,128)} %param.17) | copy-start | bytes 6148
  153.6 0.8 copy-start.28
  154.4 63.5 %all-to-all-start.1 = ((f32[512,3,256]{2,1,0:T(4,128)}), f32[512,3,256]{2,1,0:T(4,128)S(1)}, u32[]{:S(2)}, u32[]{:S(2)}) async-start(f32[512,3,256]{2,1,0:T(4,128)} %fusion.29), calls=%async_computation.1 | async-start | bytes 4194304 | tf_op jit(solution)/shard_map/all_to_all | solution.py:187
  175.0 26.3 %copy-start.24 = (f32[16,16,256]{2,1,0:T(8,128)}, f32[16,16,256]{2,1,0:T(8,128)S(1)}, u32[]{:S(2)}) copy-start(f32[16,16,256]{2,1,0:T(8,128)S(1)} %slice.234) | copy-start | bytes 786436
  182.6 15.3 %copy-start.38 = (f32[16,4,256]{2,1,0:T(4,128)}, f32[16,4,256]{2,1,0:T(4,128)S(1)}, u32[]{:S(2)}) copy-start(f32[16,4,256]{2,1,0:T(4,128)S(1)} %slice.239) | copy-start | bytes 196612
  196.8 1.0 copy-start.40
  198.4 1.1 copy-start.34
  198.5 3.6 copy-start.29
  200.3 1.8 copy-start.30
  202.4 15.5 %copy-start.11 = (f32[16,16,256]{2,1,0:T(8,128)}, f32[16,16,256]{2,1,0:T(8,128)S(1)}, u32[]{:S(2)}) copy-start(f32[16,16,256]{2,1,0:T(8,128)S(1)} %pad.220) | copy-start | bytes 786436
  217.9 1.3 copy-start.2
  219.2 15.6 %copy-start.12 = (f32[16,16,256]{2,1,0:T(8,128)S(1)}, f32[16,16,256]{2,1,0:T(8,128)}, u32[]{:S(2)}) copy-start(f32[16,16,256]{2,1,0:T(8,128)} %copy-done.11) | copy-start | bytes 786436
  225.5 0.8 copy-start.36
  225.5 16.2 %copy-start.52 = (pred[2]{0:T(512)(128)(4,1)S(1)}, pred[2]{0:T(512)(128)(4,1)}, u32[]{:S(2)}) copy-start(pred[2]{0:T(512)(128)(4,1)} %constant.235.clone.1) | copy-start | bytes 10
  234.3 10.0 %copy-start.32 = (f32[16,8,256]{2,1,0:T(8,128)S(1)}, f32[16,8,256]{2,1,0:T(8,128)}, u32[]{:S(2)}) copy-start(f32[16,8,256]{2,1,0:T(8,128)} %slice.236) | copy-start | bytes 393220
  234.4 10.1 %copy-start.31 = (f32[16,8,256]{2,1,0:T(8,128)S(1)}, f32[16,8,256]{2,1,0:T(8,128)}, u32[]{:S(2)}) copy-start(f32[16,8,256]{2,1,0:T(8,128)} %slice.237) | copy-start | bytes 393220
  234.4 10.5 %copy-start.26 = (f32[16,16,256]{2,1,0:T(8,128)S(1)}, f32[16,16,256]{2,1,0:T(8,128)}, u32[]{:S(2)}) copy-start(f32[16,16,256]{2,1,0:T(8,128)} %slice.233) | copy-start | bytes 786436
  234.4 10.6 %copy-start.25 = (f32[16,16,256]{2,1,0:T(8,128)S(1)}, f32[16,16,256]{2,1,0:T(8,128)}, u32[]{:S(2)}) copy-start(f32[16,16,256]{2,1,0:T(8,128)} %copy-done.24) | copy-start | bytes 786436
  236.6 8.8 %copy-start.35 = (f32[16,15,256]{2,1,0:T(8,128)S(1)}, f32[16,15,256]{2,1,0:T(8,128)}, u32[]{:S(2)}) copy-start(f32[16,15,256]{2,1,0:T(8,128)} %get-tuple-element.62) | copy-start | bytes 737284
  273.7 51.1 %all-to-all-start.3 = ((f32[32,16,256]{2,1,0:T(8,128)}), f32[32,16,256]{2,1,0:T(8,128)}, u32[]{:S(2)}, u32[]{:S(2)}) async-start(f32[32,16,256]{2,1,0:T(8,128)} %copy.226), calls=%async_computation.3 | async-start | bytes 1048576 | tf_op jit(solution)/shard_map/all_to_all | solution.py:202
  283.6 51.4 %copy-start.43 = (f32[512,16]{0,1:T(8,128)S(1)}, f32[512,16]{0,1:T(8,128)}, u32[]{:S(2)}) copy-start(f32[512,16]{0,1:T(8,128)} %get-tuple-element.54) | copy-start | bytes 98308
  284.0 99.9 %copy-start.7 = (f32[512,256]{1,0:T(8,128)S(1)}, f32[512,256]{1,0:T(8,128)}, u32[]{:S(2)}) copy-start(f32[512,256]{1,0:T(8,128)} %broadcast_add_fusion.1) | copy-start | bytes 1572868
  284.0 99.9 %copy-start.14 = (f32[512,16]{1,0:T(8,128)S(1)}, f32[512,16]{1,0:T(8,128)}, u32[]{:S(2)}) copy-start(f32[512,16]{1,0:T(8,128)} %copy-done.13) | copy-start | bytes 98308
  324.8 59.1 %all-to-all-start.2 = ((f32[512,3,256]{2,1,0:T(4,128)}), f32[512,3,256]{2,1,0:T(4,128)}, u32[]{:S(2)}, u32[]{:S(2)}) async-start(f32[512,3,256]{2,1,0:T(4,128)} %bitcast.137), calls=%async_computation.2 | async-start | bytes 4194304 | tf_op jit(solution)/shard_map/all_to_all | solution.py:195
  334.7 261.7 %reduce-scatter.2.cloned.1.call-start = ((), (), s32[]{:S(2)}) async-start(), calls=%async_computation.6 | async-start | bytes 4718592 | tf_op jit(solution)/shard_map/reduce_scatter | solution.py:218
  337.9 69.6 %copy-start.51 = (f32[16]{0:T(128)S(1)}, f32[16]{0:T(128)}, u32[]{:S(2)}) copy-start(f32[16]{0:T(128)} %copy-done.50) | copy-start | bytes 196
  337.9 69.8 %copy-start.5 = (f32[512,256]{1,0:T(8,128)S(1)}, f32[512,256]{1,0:T(8,128)}, u32[]{:S(2)}) copy-start(f32[512,256]{1,0:T(8,128)} %broadcast_add_fusion) | copy-start | bytes 1572868
  337.9 69.8 %copy-start.8 = (f32[512,256]{1,0:T(8,128)S(1)}, f32[512,256]{1,0:T(8,128)}, u32[]{:S(2)}) copy-start(f32[512,256]{1,0:T(8,128)} %broadcast_add_fusion.1) | copy-start | bytes 1572868
  337.9 69.8 %copy-start.15 = (f32[512,16]{1,0:T(8,128)S(1)}, f32[512,16]{1,0:T(8,128)}, u32[]{:S(2)}) copy-start(f32[512,16]{1,0:T(8,128)} %copy-done.13) | copy-start | bytes 98308
  337.9 69.8 %copy-start.17 = (f32[512,16]{1,0:T(8,128)S(1)}, f32[512,16]{1,0:T(8,128)}, u32[]{:S(2)}) copy-start(f32[512,16]{1,0:T(8,128)} %copy-done.16) | copy-start | bytes 98308
  428.6 8.5 %copy-start.20 = (f32[512,16]{1,0:T(8,128)S(1)}, f32[512,16]{1,0:T(8,128)}, u32[]{:S(2)}) copy-start(f32[512,16]{1,0:T(8,128)} %copy-done.18) | copy-start | bytes 98308
  428.6 8.5 %copy-start.23 = (f32[512,16]{1,0:T(8,128)S(1)}, f32[512,16]{1,0:T(8,128)}, u32[]{:S(2)}) copy-start(f32[512,16]{1,0:T(8,128)} %copy-done.21) | copy-start | bytes 98308
  428.6 8.5 %copy-start.27 = (f32[512,256]{1,0:T(8,128)S(1)}, f32[512,256]{1,0:T(8,128)}, u32[]{:S(2)}) copy-start(f32[512,256]{1,0:T(8,128)} %bitcast_multiply_fusion) | copy-start | bytes 1572868
  428.6 8.5 %copy-start.33 = (f32[512,16]{1,0:T(8,128)S(1)}, f32[512,16]{1,0:T(8,128)}, u32[]{:S(2)}) copy-start(f32[512,16]{1,0:T(8,128)} %copy.231) | copy-start | bytes 98308
  437.1 37.2 %copy-start.47 = (s32[1,512,1]{1,2,0:T(1,128)S(1)}, s32[1,512,1]{1,2,0:T(1,128)}, u32[]{:S(2)}) copy-start(s32[1,512,1]{1,2,0:T(1,128)} %param.15) | copy-start | bytes 6148
  437.1 37.2 %copy-start.49 = (pred[512]{0:T(512)(128)(4,1)S(1)}, pred[512]{0:T(512)(128)(4,1)}, u32[]{:S(2)}) copy-start(pred[512]{0:T(512)(128)(4,1)} %copy-done.48) | copy-start | bytes 1540
  475.2 51.0 %copy-start.39 = (s32[1,512,1,16]{1,3,2,0:T(8,128)S(1)}, s32[1,512,1,16]{1,3,2,0:T(8,128)}, u32[]{:S(2)}) copy-start(s32[1,512,1,16]{1,3,2,0:T(8,128)} %param.14) | copy-start | bytes 98308
  475.5 51.3 %copy-start.41 = (f32[53,1024]{1,0:T(8,128)S(1)}, f32[53,1024]{1,0:T(8,128)}, u32[]{:S(2)}) copy-start(f32[53,1024]{1,0:T(8,128)} %param.10) | copy-start | bytes 651268
  475.5 51.5 %copy-start.42 = (f32[53,1024]{1,0:T(8,128)S(1)}, f32[53,1024]{1,0:T(8,128)}, u32[]{:S(2)}) copy-start(f32[53,1024]{1,0:T(8,128)} %param.11) | copy-start | bytes 651268
  475.5 95.3 %copy-start.53 = (u32[256]{0:T(256)S(1)}, u32[256]{0:T(256)}, u32[]{:S(2)}) copy-start(u32[256]{0:T(256)} %constant.393) | copy-start | bytes 3076
  475.5 120.2 %copy-start.37 = (f32[16,3,256]{2,1,0:T(4,128)S(1)}, f32[16,3,256]{2,1,0:T(4,128)}, u32[]{:S(2)}) copy-start(f32[16,3,256]{2,1,0:T(4,128)} %copy-done.36) | copy-start | bytes 147460
  475.5 120.8 %copy-start.9 = (f32[53,1024]{0,1:T(8,128)S(1)}, f32[53,1024]{0,1:T(8,128)}, u32[]{:S(2)}) copy-start(f32[53,1024]{0,1:T(8,128)} %copy.209) | copy-start | bytes 651268
  479.6 120.8 %copy-start.1 = (s32[32,32,1,2]{1,3,2,0:T(2,128)S(1)}, s32[32,32,1,2]{1,3,2,0:T(2,128)}, u32[]{:S(2)}) copy-start(s32[32,32,1,2]{1,3,2,0:T(2,128)} %param.16) | copy-start | bytes 24580
Sparse Core Ops, SparseCore 0:
  9.9 37.2 all-gather.1
  526.3 36.1 reduce-scatter.1
where the time goes:
time: 620 us; the launch traced here: 608 us
  other arithmetic  267 us (43%)
  local copies, waits for them, and re-layouts  109 us (18%)
  matrix products  64.1 us (10%)
  waiting for transfers between devices  53 us (9%)
  starting transfers between devices  50.6 us (8%)
  between operations  40.5 us (7%)
  blocking collectives  23.6 us (4%)
    dot_general x3, matrix products, render_tiles(): jnp.einsum('crk,rkp->rcp', colour, weight, precision=lax.Precision.HIGHEST)  62.4 us
    scatter-add x1, other arithmetic, render_tiles(): picked = jnp.take(cell_params, list_ids, axis=1)  46.5 us
    all_to_all x1, waiting for transfers between devices, per_device(): lax.all_to_all(grad_colour.reshape(rows_total, 3, pixels), 'cell', split_...  46 us
    scatter-add x1, other arithmetic, per_device(): touch_count = jnp.zeros((cell_params.shape[1],), jnp.float32).at[local_id...  43.5 us
    scatter-add x1, other arithmetic, merge_tiles(): jnp.take_along_axis(colour_t, tile_order[:, :, None, None], axis=1)  38.9 us
    gather x2, local copies, waits for them, and re-layouts, render_tiles(): picked = jnp.take(cell_params, list_ids, axis=1)  33.6 us
    reduce_sum x1, other arithmetic, render_tiles(): anchor_y[:, None, None] + off_y[None, None, :] - screen_y[:, :, None]  29.2 us
    scatter-add x1, other arithmetic, merge_tiles(): through_s = jnp.take_along_axis(through_t, tile_order[:, :, None], axis=1)  26.9 us
  transfers between devices with their start and end apart: 6, of which 2 were waited for; matrix products, arithmetic and copies ran while one was open for 28% of the time, Pallas kernels for 0%

commit v1 on v0

v1 whole, which is shorter than its diff:
```python
import jax
import jax.numpy as jnp
from jax import lax
from jax.experimental import pallas as pl
from jax.experimental.pallas import tpu as pltpu
from jax.sharding import PartitionSpec as P

CELLS = 32
VIEWS = 8
HALF_VIEWS = VIEWS // 2
HOME = 1024
OWN = 16
ROWS = 512
PIX = 256
TSIDE = 16
LISTS = 2 * CELLS
SUB = 8
LANES = 128
HIGHS = VIEWS * SUB
F32 = jnp.float32
BF16 = jnp.bfloat16
LARGE = 1e38

band_zero = 0.28209479177387814
band_one = 0.4886025119029199
band_two = (
    1.0925484305920792,
    -1.0925484305920792,
    0.31539156525252005,
    -1.0925484305920792,
    0.5462742152960396,
)
band_three = (
    -0.5900435899266435,
    2.890611442640554,
    -0.4570457994644658,
    0.3731763325901154,
    -0.4570457994644658,
    1.445305721320277,
    -0.5900435899266435,
)
beta_one = 0.9
beta_two = 0.999
learn_rate = 0.01
adam_eps = 1e-08
adam_step = 10.0


def iota(shape, axis):
    return lax.broadcasted_iota(jnp.int32, shape, axis)


def camera_values(cam_ref, which):
    return [[cam_ref[which, row : row + 1, k : k + 1] for k in range(4)] for row in range(2)]


def basis_column(camera):
    a, b = camera
    nx = a[1] * b[2] - a[2] * b[1]
    ny = a[2] * b[0] - a[0] * b[2]
    nz = a[0] * b[1] - a[1] * b[0]
    norm = jnp.sqrt(nx * nx + ny * ny + nz * nz)
    x, y, z = nx / norm, ny / norm, nz / norm
    xx, yy, zz = x * x, y * y, z * z
    terms = [
        x * 0.0 + band_zero,
        -band_one * y,
        band_one * z,
        -band_one * x,
        band_two[0] * x * y,
        band_two[1] * y * z,
        band_two[2] * (2.0 * zz - xx - yy),
        band_two[3] * x * z,
        band_two[4] * (xx - yy),
        band_three[0] * y * (3.0 * xx - yy),
        band_three[1] * x * y * z,
        band_three[2] * y * (4.0 * zz - xx - yy),
        band_three[3] * z * (2.0 * zz - 3.0 * xx - 3.0 * yy),
        band_three[4] * x * (4.0 * zz - xx - yy),
        band_three[5] * z * (xx - yy),
        band_three[6] * x * (xx - 3.0 * yy),
    ]
    row = iota((16, 1), 0)
    column = jnp.zeros((16, 1), F32)
    for at, term in enumerate(terms):
        column = jnp.where(row == at, term, column)
    return column


def split3(x):
    high = x.astype(BF16)
    rest = x - high.astype(F32)
    mid = rest.astype(BF16)
    low = (rest - mid.astype(F32)).astype(BF16)
    return high, mid, low


def dot(a, b, dims=((1,), (0,))):
    return lax.dot_general(a, b, (dims, ((), ())), preferred_element_type=F32)


def rows_to_lists(x):
    t = x.T
    return jnp.concatenate([t[:LISTS], t[LISTS:]], axis=1)


def lists_to_rows(x):
    t = x.T
    return jnp.concatenate([t[:64], t[64:]], axis=1)


def step_kernel(
    g_ref,
    cam_ref,
    tgt_ref,
    ids_ref,
    cnt_ref,
    isl_ref,
    ord_ref,
    rend_ref,
    gout_ref,
    tab_send,
    tab_recv,
    fwd_send,
    fwd_recv,
    bwd_send,
    bwd_recv,
    grad_send,
    grad_recv,
    oh_ref,
    hi_ref,
    v_ref,
    ex_ref,
    ey_ref,
    dy_ref,
    w_ref,
    rho_ref,
    part_ref,
    pre_ref,
    behind_ref,
    gl_ref,
    acc_ref,
    lhs_ref,
    sem_ts,
    sem_tr,
    sem_fs,
    sem_fr,
    sem_bs,
    sem_br,
    sem_gs,
    sem_gr,
):
    me_c = lax.axis_index("cell")
    me_v = lax.axis_index("view")

    def peer_c(d):
        return lax.rem(me_c + d, CELLS)

    def peer_v(d):
        return lax.rem(me_v + d, VIEWS)

    barrier = pltpu.get_barrier_semaphore()

    def greet_cell(d, carry):
        pl.semaphore_signal(
            barrier, inc=1, device_id=(peer_c(d), me_v), device_id_type=pl.DeviceIdType.MESH
        )
        return carry

    def greet_view(d, carry):
        pl.semaphore_signal(
            barrier, inc=1, device_id=(me_c, peer_v(d)), device_id_type=pl.DeviceIdType.MESH
        )
        return carry

    lax.fori_loop(1, VIEWS, greet_view, 0)
    lax.fori_loop(1, CELLS, greet_cell, 0)

    centre = [g_ref[k : k + 1, :] for k in range(3)]
    inv_var = jnp.exp(-2.0 * g_ref[3:4, :])
    opacity = 1.0 / (1.0 + jnp.exp(-g_ref[4:5, :]))
    for which in range(2):
        camera = camera_values(cam_ref, which)
        column = basis_column(camera)
        screen = [
            row[0] * centre[0] + row[1] * centre[1] + row[2] * centre[2] + row[3] for row in camera
        ]
        colour = [
            0.5 + jnp.sum(g_ref[5 + 16 * ch : 21 + 16 * ch, :] * column, axis=0, keepdims=True)
            for ch in range(3)
        ]
        table = jnp.concatenate(
            screen + [inv_var, opacity] + colour + [jnp.zeros((1, HOME), F32)], axis=0
        )
        table = jnp.clip(table, -LARGE, LARGE)
        tab_send[which] = jnp.where(table == table, table, 0.0)

    pl.semaphore_wait(barrier, VIEWS - 1 + CELLS - 1)

    def table_copy(d):
        to = peer_v(d)
        return pltpu.make_async_remote_copy(
            src_ref=tab_send.at[to // HALF_VIEWS],
            dst_ref=tab_recv.at[me_v],
            send_sem=sem_ts.at[d],
            recv_sem=sem_tr.at[me_v],
            device_id=(me_c, to),
            device_id_type=pl.DeviceIdType.MESH,
        )

    def table_start(d, carry):
        table_copy(d).start()
        return carry

    lax.fori_loop(1, VIEWS, table_start, 0)
    tab_recv[me_v] = tab_send[me_v // HALF_VIEWS]

    lane = iota((1, LANES), 1)
    mine = isl_ref[me_c]
    offsets = jnp.concatenate([mine[0:1], mine[1:2], mine[0:1], mine[1:2]], axis=1)
    wanted = jnp.where(offsets >= 0, lax.rem(lane, CELLS) * OWN + offsets, -1)
    pick = (iota((ROWS, LANES), 0) == wanted).astype(F32).astype(BF16)
    all_ids = ids_ref[...]
    packed = jnp.concatenate(
        [
            (all_ids // LANES).astype(F32),
            lax.rem(all_ids, LANES).astype(F32),
            jnp.broadcast_to(cnt_ref[...].astype(F32), (16, ROWS)),
        ],
        axis=0,
    ).astype(BF16)
    picked = dot(packed, pick)
    left = iota((SUB, LANES), 1) < LISTS
    high = jnp.where(left, picked[0:8], picked[8:16])
    low = jnp.where(left, picked[16:24], picked[24:32])
    slot = iota((SUB, LANES), 0) + jnp.where(left, 0, SUB)
    live = slot.astype(F32) < picked[32:40]
    high = jnp.where(live, high, -1.0)
    hi_ref[...] = high
    for kk in range(SUB):
        hot = (iota((LANES, LANES), 0).astype(F32) == low[kk : kk + 1]).astype(F32).astype(BF16)
        for part in range(3):
            oh_ref[part * LANES : (part + 1) * LANES, kk * LANES : (kk + 1) * LANES] = hot

    def table_wait(d, carry):
        pltpu.make_async_remote_copy(
            src_ref=tab_send.at[0],
            dst_ref=tab_recv.at[peer_v(d)],
            send_sem=sem_ts.at[d],
            recv_sem=sem_tr.at[peer_v(d)],
            device_id=(me_c, peer_v(d)),
            device_id_type=pl.DeviceIdType.MESH,
        ).wait_recv()
        return carry

    lax.fori_loop(1, VIEWS, table_wait, 0)

    blocks = []
    for home in range(VIEWS):
        for at in range(SUB):
            value = tab_recv[home, :, at * LANES : (at + 1) * LANES]
            blocks.append(value)
    parts = split3(jnp.concatenate(blocks, axis=0))
    lhs = jnp.concatenate(parts, axis=1)
    chosen = []
    for pair in range(4):
        got = dot(lhs, oh_ref[:, pair * 256 : (pair + 1) * 256])
        for side in range(2):
            hi = hi_ref[2 * pair + side : 2 * pair + side + 1, :]
            total = jnp.zeros((SUB, LANES), F32)
            for at in range(HIGHS):
                total = total + jnp.where(
                    hi == float(at), got[at * SUB : (at + 1) * SUB, side * LANES : (side + 1) * LANES], 0.0
                )
            chosen.append(total)
    lists = rows_to_lists(jnp.concatenate(chosen, axis=0))
    fwd_send[:, 0, :] = lists[:CELLS]
    fwd_send[:, 1, :] = lists[CELLS:]

    def cell_copy(source, target, send, recv, d):
        return pltpu.make_async_remote_copy(
            src_ref=source.at[peer_c(d)],
            dst_ref=target.at[me_c],
            send_sem=send.at[d],
            recv_sem=recv.at[me_c],
            device_id=(peer_c(d), me_v),
            device_id_type=pl.DeviceIdType.MESH,
        )

    def cell_arrived(source, target, send, recv, d):
        return pltpu.make_async_remote_copy(
            src_ref=source.at[peer_c(d)],
            dst_ref=target.at[peer_c(d)],
            send_sem=send.at[d],
            recv_sem=recv.at[peer_c(d)],
            device_id=(peer_c(d), me_v),
            device_id_type=pl.DeviceIdType.MESH,
        )

    def fwd_start(d, carry):
        cell_copy(fwd_send, fwd_recv, sem_fs, sem_fr, d).start()
        return carry

    lax.fori_loop(1, CELLS, fwd_start, 0)
    fwd_recv[me_c] = fwd_send[me_c]

    both = jnp.concatenate([isl_ref[:, 0, :], isl_ref[:, 1, :]], axis=0).astype(F32)
    at_me = jnp.where(iota((LISTS, CELLS), 1) == me_c, both, 0.0)
    tile_half = jnp.sum(at_me, axis=1, keepdims=True)
    tile_col = jnp.concatenate([tile_half, tile_half], axis=0)
    eye = iota((LANES, LANES), 0) == iota((LANES, LANES), 1)
    tile_row = jnp.sum(jnp.where(eye, tile_col, 0.0), axis=0, keepdims=True)
    in_tile = (iota((OWN, LANES), 0).astype(F32) == tile_row).astype(F32)
    order = ord_ref[...].reshape(OWN, CELLS)
    cell_lane = lax.rem(iota((OWN, LANES), 1), CELLS)
    rank = jnp.zeros((OWN, LANES), F32)
    for at in range(CELLS):
        rank = jnp.where(order[:, at : at + 1] == cell_lane, float(at), rank)
    rank_row = jnp.sum(in_tile * rank, axis=0, keepdims=True)
    key_row = 2.0 * rank_row + jnp.where(lane < LISTS, 0.0, 1.0)
    key_col = jnp.sum(jnp.where(eye, key_row, 0.0), axis=1, keepdims=True)
    same = (tile_col == tile_row) & (tile_row >= 0.0)
    ahead = (same & (key_col < key_row)).astype(F32).astype(BF16)
    after = (same & (key_col > key_row)).astype(F32).astype(BF16)
    ahead3 = jnp.concatenate([ahead] * 3, axis=0)
    after3 = jnp.concatenate([after] * 3, axis=0)
    in_tile_b = in_tile.astype(BF16)
    in_tile3 = jnp.concatenate([in_tile_b] * 3, axis=1)
    in_tile3v = jnp.concatenate([in_tile_b] * 3, axis=0)
    tile_int = tile_row.astype(jnp.int32)
    window = lax.rem(me_v, HALF_VIEWS) * ROWS + me_c * OWN + tile_int
    side_at = iota((TSIDE, LANES), 0).astype(F32) + 0.5
    place_x = (lax.rem(window, 32) * TSIDE).astype(F32) + side_at
    place_y = ((window // 32) * TSIDE).astype(F32) + side_at
    acc_ref[...] = jnp.zeros_like(acc_ref)

    def fwd_wait(d, carry):
        cell_arrived(fwd_send, fwd_recv, sem_fs, sem_fr, d).wait_recv()
        return carry

    lax.fori_loop(1, CELLS, fwd_wait, 0)
    v_ref[...] = lists_to_rows(
        jnp.concatenate([fwd_recv[:, 0, :], fwd_recv[:, 1, :]], axis=0)
    )

    def value(kk, j):
        return v_ref[kk * SUB + j : kk * SUB + j + 1, :]

    for kk in range(SUB):
        inv = -0.5 * value(kk, 2)
        dx = place_x - value(kk, 0)
        dy = place_y - value(kk, 1)
        ex_ref[kk] = value(kk, 3) * jnp.exp(inv * (dx * dx))
        ey_ref[kk] = jnp.exp(inv * (dy * dy))
        dy_ref[kk] = dy

    def forward(i, carry):
        rows = pl.ds(pl.multiple_of(i * 32, 32), 32)
        through = jnp.ones((32, LANES), F32)
        second = jnp.ones((32, LANES), F32)
        first = through
        sums = [jnp.zeros((32, LANES), F32) for ch in range(3)]
        for kk in range(SUB):
            ex = ex_ref[kk]
            alpha = jnp.concatenate(
                [ex * ey_ref[kk, pl.ds(2 * i + at, 1), :] for at in range(2)], axis=0
            )
            keep = 1.0 - alpha
            weight = alpha * through
            w_ref[kk, rows, :] = weight
            rho_ref[kk, rows, :] = alpha / keep
            for ch in range(3):
                sums[ch] = sums[ch] + weight * value(kk, 4 + ch)
            through = through * keep
            if kk < 4:
                first = through
            else:
                second = second * keep
        for ch in range(3):
            part_ref[ch, rows, :] = sums[ch]
        pre_ref[rows, :] = jnp.log(first) + jnp.log(second)
        return carry

    lax.fori_loop(0, 8, forward, 0)

    prefix = jnp.exp(dot(jnp.concatenate(split3(pre_ref[...]), axis=1), ahead3))
    pre_ref[...] = prefix
    owed = jnp.zeros((PIX, LANES), F32)
    for ch in range(3):
        seen = prefix * part_ref[ch]
        image = dot(in_tile3, jnp.concatenate(split3(seen), axis=1), ((1,), (1,)))
        rend_ref[pl.ds(2 * ch, OWN, stride=6), :] = image[:, :LANES]
        rend_ref[pl.ds(2 * ch + 1, OWN, stride=6), :] = image[:, LANES:]
        miss = image - tgt_ref[ch].astype(F32)
        miss3 = jnp.concatenate(split3(miss), axis=0)
        pulled = dot(miss3, in_tile3v, ((0,), (0,)))
        gl_ref[ch] = pulled
        owed = owed + seen * pulled
    behind_ref[...] = dot(jnp.concatenate(split3(owed), axis=1), after3)

    def backward(i, carry):
        rows = pl.ds(pl.multiple_of(i * 32, 32), 32)
        prefix = pre_ref[rows, :]
        behind = behind_ref[rows, :]
        pulled = [gl_ref[ch, rows, :] for ch in range(3)]
        for kk in reversed(range(SUB)):
            weight = prefix * w_ref[kk, rows, :]
            gain = (
                pulled[0] * value(kk, 4) + pulled[1] * value(kk, 5) + pulled[2] * value(kk, 6)
            )
            owed = weight * gain
            pull = owed - behind * rho_ref[kk, rows, :]
            behind = behind + owed
            up, down = pull[:16], pull[16:]
            dy_up = dy_ref[kk, pl.ds(2 * i, 1), :]
            dy_down = dy_ref[kk, pl.ds(2 * i + 1, 1), :]
            acc_ref[kk, 0] += up + down
            along = up * dy_up
            along_down = down * dy_down
            acc_ref[kk, 1] += along + along_down
            acc_ref[kk, 2] += along * dy_up + along_down * dy_down
            for ch in range(3):
                tint = weight * pulled[ch]
                acc_ref[kk, 3 + ch] += tint[:16] + tint[16:]
        return carry

    lax.fori_loop(0, 8, backward, 0)

    results = []
    for kk in range(SUB):
        dx = place_x - value(kk, 0)
        inv = value(kk, 2)
        base = acc_ref[kk, 0]
        base_x = base * dx

        def total(x):
            return jnp.sum(x, axis=0, keepdims=True)

        results += [
            inv * total(base_x),
            inv * total(acc_ref[kk, 1]),
            inv * total(base_x * dx + acc_ref[kk, 2]),
            (1.0 - value(kk, 3)) * total(base),
            total(acc_ref[kk, 3]),
            total(acc_ref[kk, 4]),
            total(acc_ref[kk, 5]),
            jnp.zeros((1, LANES), F32),
        ]
    lists = rows_to_lists(jnp.concatenate(results, axis=0))
    bwd_send[:, 0, :] = lists[:CELLS]
    bwd_send[:, 1, :] = lists[CELLS:]

    def bwd_start(d, carry):
        cell_copy(bwd_send, bwd_recv, sem_bs, sem_br, d).start()
        return carry

    lax.fori_loop(1, CELLS, bwd_start, 0)
    bwd_recv[me_c] = bwd_send[me_c]

    def bwd_wait(d, carry):
        cell_arrived(bwd_send, bwd_recv, sem_bs, sem_br, d).wait_recv()
        return carry

    lax.fori_loop(1, CELLS, bwd_wait, 0)

    grads = lists_to_rows(jnp.concatenate([bwd_recv[:, 0, :], bwd_recv[:, 1, :]], axis=0))
    last = iota((SUB, LANES), 0) == SUB - 1
    for kk in range(SUB):
        hi = hi_ref[kk : kk + 1, :]
        piece = split3(jnp.where(last, 1.0, grads[kk * SUB : (kk + 1) * SUB]))
        piece = [x.astype(F32) for x in piece]
        for at in range(0, HIGHS, 2):
            here, there = hi == float(at), hi == float(at + 1)
            for part in range(3):
                lhs_ref[part, at * SUB : (at + 2) * SUB, kk * LANES : (kk + 1) * LANES] = (
                    jnp.concatenate(
                        [jnp.where(here, piece[part], 0.0), jnp.where(there, piece[part], 0.0)],
                        axis=0,
                    ).astype(BF16)
                )
    hot = oh_ref[0:LANES, :]
    spread = dot(lhs_ref[0], hot, ((1,), (1,)))
    spread = spread + dot(lhs_ref[1], hot, ((1,), (1,)))
    spread = spread + dot(lhs_ref[2], hot, ((1,), (1,)))
    for home in range(VIEWS):
        for at in range(SUB):
            row = (home * SUB + at) * SUB
            grad_send[home, :, at * LANES : (at + 1) * LANES] = spread[row : row + SUB]

    def grad_start(d, carry):
        to = peer_v(d)
        pltpu.make_async_remote_copy(
            src_ref=grad_send.at[to],
            dst_ref=grad_recv.at[me_v],
            send_sem=sem_gs.at[d],
            recv_sem=sem_gr.at[me_v],
            device_id=(me_c, to),
            device_id_type=pl.DeviceIdType.MESH,
        ).start()
        return carry

    lax.fori_loop(1, VIEWS, grad_start, 0)
    grad_recv[me_v] = grad_send[me_v]

    def grad_arrived(d):
        return pltpu.make_async_remote_copy(
            src_ref=grad_send.at[peer_v(d)],
            dst_ref=grad_recv.at[peer_v(d)],
            send_sem=sem_gs.at[d],
            recv_sem=sem_gr.at[peer_v(d)],
            device_id=(me_c, peer_v(d)),
            device_id_type=pl.DeviceIdType.MESH,
        )

    def grad_wait(d, carry):
        grad_arrived(d).wait_recv()
        return carry

    lax.fori_loop(1, VIEWS, grad_wait, 0)
    gout_ref[0] = (grad_recv[0] + grad_recv[1]) + (grad_recv[2] + grad_recv[3])
    gout_ref[1] = (grad_recv[4] + grad_recv[5]) + (grad_recv[6] + grad_recv[7])

    def sent_view(d, carry):
        table_copy(d).wait_send()
        grad_arrived(d).wait_send()
        return carry

    def sent_cell(d, carry):
        cell_copy(fwd_send, fwd_recv, sem_fs, sem_fr, d).wait_send()
        cell_copy(bwd_send, bwd_recv, sem_bs, sem_br, d).wait_send()
        return carry

    lax.fori_loop(1, VIEWS, sent_view, 0)
    lax.fori_loop(1, CELLS, sent_cell, 0)


def adam_kernel(grad_ref, cam_ref, g_ref, one_ref, two_ref, new_g, new_one, new_two):
    touched = grad_ref[0, 7:8, :] + grad_ref[1, 7:8, :] > 0.5
    cameras = [camera_values(cam_ref, which) for which in range(2)]
    columns = [basis_column(camera) for camera in cameras]
    fix_one = 1.0 / (1.0 - beta_one**adam_step)
    fix_two = 1.0 / (1.0 - beta_two**adam_step)

    def update(rows, grad):
        first = beta_one * one_ref[rows, :] + (1.0 - beta_one) * grad
        second = beta_two * two_ref[rows, :] + (1.0 - beta_two) * grad * grad
        change = learn_rate * (first * fix_one) / (jnp.sqrt(second * fix_two) + adam_eps)
        new_g[rows, :] = jnp.where(touched, g_ref[rows, :] - change, g_ref[rows, :])
        new_one[rows, :] = jnp.where(touched, first, one_ref[rows, :])
        new_two[rows, :] = jnp.where(touched, second, two_ref[rows, :])

    small = []
    for k in range(3):
        small.append(
            sum(
                cameras[which][row][k] * grad_ref[which, row : row + 1, :]
                for which in range(2)
                for row in range(2)
            )
        )
    for j in (2, 3):
        small.append(grad_ref[0, j : j + 1, :] + grad_ref[1, j : j + 1, :])
    update(slice(0, 5), jnp.concatenate(small, axis=0))
    for ch in range(3):
        j = 4 + ch
        update(
            slice(5 + 16 * ch, 21 + 16 * ch),
            columns[0] * grad_ref[0, j : j + 1, :] + columns[1] * grad_ref[1, j : j + 1, :],
        )


def per_device(
    gaussians,
    moment_one,
    moment_two,
    cameras,
    target,
    gauss_ids,
    tile_counts,
    intersection_slots,
    depth_order,
):
    vmem = pl.BlockSpec(memory_space=pltpu.VMEM)
    sems = pltpu.SemaphoreType.DMA
    rendered, grads = pl.pallas_call(
        step_kernel,
        out_shape=(
            jax.ShapeDtypeStruct((96, LANES), F32),
            jax.ShapeDtypeStruct((2, SUB, HOME), F32),
        ),
        in_specs=[vmem] * 7,
        out_specs=(vmem, vmem),
        scratch_shapes=[
            pltpu.VMEM((2, SUB, HOME), F32),
            pltpu.VMEM((VIEWS, SUB, HOME), F32),
            pltpu.VMEM((CELLS, 2, LANES), F32),
            pltpu.VMEM((CELLS, 2, LANES), F32),
            pltpu.VMEM((CELLS, 2, LANES), F32),
            pltpu.VMEM((CELLS, 2, LANES), F32),
            pltpu.VMEM((VIEWS, SUB, HOME), F32),
            pltpu.VMEM((VIEWS, SUB, HOME), F32),
            pltpu.VMEM((3 * LANES, SUB * LANES), BF16),
            pltpu.VMEM((SUB, LANES), F32),
            pltpu.VMEM((64, LANES), F32),
            pltpu.VMEM((SUB, TSIDE, LANES), F32),
            pltpu.VMEM((SUB, TSIDE, LANES), F32),
            pltpu.VMEM((SUB, TSIDE, LANES), F32),
            pltpu.VMEM((SUB, PIX, LANES), F32),
            pltpu.VMEM((SUB, PIX, LANES), F32),
            pltpu.VMEM((3, PIX, LANES), F32),
            pltpu.VMEM((PIX, LANES), F32),
            pltpu.VMEM((PIX, LANES), F32),
            pltpu.VMEM((3, PIX, LANES), F32),
            pltpu.VMEM((SUB, 6, TSIDE, LANES), F32),
            pltpu.VMEM((3, HIGHS * SUB, SUB * LANES), BF16),
            sems((VIEWS,)),
            sems((VIEWS,)),
            sems((CELLS,)),
            sems((CELLS,)),
            sems((CELLS,)),
            sems((CELLS,)),
            sems((VIEWS,)),
            sems((VIEWS,)),
        ],
        compiler_params=pltpu.CompilerParams(
            collective_id=0, has_side_effects=True, vmem_limit_bytes=40 * 1024 * 1024
        ),
        name="splat_step",
    )(
        gaussians,
        cameras,
        jnp.transpose(target[:, 0], (1, 0, 2)),
        jnp.transpose(gauss_ids[0, :, 0, :], (1, 0)),
        tile_counts.reshape(1, ROWS),
        jnp.transpose(intersection_slots[:, :, 0, :], (0, 2, 1)),
        depth_order,
    )
    shape = jax.ShapeDtypeStruct(gaussians.shape, F32)
    new_gaussians, new_one, new_two = pl.pallas_call(
        adam_kernel,
        out_shape=(shape, shape, shape),
        in_specs=[vmem] * 5,
        out_specs=(vmem,) * 3,
        compiler_params=pltpu.CompilerParams(vmem_limit_bytes=20 * 1024 * 1024),
        name="adam",
    )(grads, cameras, gaussians, moment_one, moment_two)
    return (rendered.reshape(OWN, 1, 3, PIX), new_gaussians, new_one, new_two)


def solution(mesh):
    placed = (
        P(None, ("cell", "view")),
        P(None, ("cell", "view")),
        P(None, ("cell", "view")),
        P(),
        P("cell", "view", None, None),
        P("cell", None, "view", None),
        P("cell", None, "view"),
        P(None, None, "view", None),
        P("cell", "view", None),
    )
    return jax.shard_map(
        per_device,
        mesh=mesh,
        in_specs=placed,
        out_specs=(
            P("cell", "view", None, None),
            P(None, ("cell", "view")),
            P(None, ("cell", "view")),
            P(None, ("cell", "view")),
        ),
        check_vma=False,
    )
```

time: 620 us -> 50.8 us (0.08)
  the two profiles are of different devices: /device:TPU:32 before, /device:TPU:1 now
where the time goes in v1:
time: 50.8 us; the launch traced here: 50.4 us
  Pallas kernels  43.6 us (86%)
  local copies, waits for them, and re-layouts  6.13 us (12%)
  between operations  0.68 us (1%)
    pallas_call x1, Pallas kernels, per_device(): pl.pallas_call(step_kernel, out_shape=(jax.ShapeDtypeStruct((96, LANES),...  41.2 us
    unnamed x19, local copies, waits for them, and re-layouts  6.13 us
    pallas_call x1, Pallas kernels, per_device(): pl.pallas_call(adam_kernel, out_shape=(shape, shape, shape), in_specs=[vm...  2.4 us

profile of v1, /device:TPU:1, one launch (start us, length us, event | category | flops | bytes accessed | tf_op | source)
XLA Modules:
  0.0 50.4 jit_solution(1711601291895163930)
XLA Ops:
  0.6 0.0 copy-start.8
  0.6 0.0 copy-start.7
  0.7 0.7 %copy-done.8 = s32[1,512,1]{1,2,0:T(1,128)S(1)} copy-done((s32[1,512,1]{1,2,0:T(1,128)S(1)}, s32[1,512,1]{1,2,0:T(1,128)}, u32[]{:S(2)}) %copy-start.8) | copy-done | bytes 2072
  1.3 0.0 copy-done.7
  1.3 0.0 copy-start
  1.3 0.9 %copy-done = f32[53,1024]{1,0:T(8,128)S(1)} copy-done((f32[53,1024]{1,0:T(8,128)S(1)}, f32[53,1024]{1,0:T(8,128)}, u32[]{:S(2)}) %copy-start) | copy-done | bytes 217112
  2.3 0.0 copy-start.3
  2.3 0.8 %copy-done.3 = s32[1,512,1,16]{1,3,2,0:T(8,128)S(1)} copy-done((s32[1,512,1,16]{1,3,2,0:T(8,128)S(1)}, s32[1,512,1,16]{1,3,2,0:T(8,128)}, u32[]{:S(2)}) %copy-start.3) | copy-done | bytes 32792
  3.0 0.0 copy-start.4
  3.0 0.8 %copy-done.4 = s32[32,32,1,2]{1,3,2,0:T(2,128)S(1)} copy-done((s32[32,32,1,2]{1,3,2,0:T(2,128)S(1)}, s32[32,32,1,2]{1,3,2,0:T(2,128)}, u32[]{:S(2)}) %copy-start.4) | copy-done | bytes 8216
  3.8 0.0 copy-start.5
  3.8 0.7 %copy-done.5 = bf16[16,1,3,256]{3,0,2,1:T(8,128)(2,1)S(1)} copy-done((bf16[16,1,3,256]{3,0,2,1:T(8,128)(2,1)S(1)}, bf16[16,1,3,256]{3,0,2,1:T(8,128)(2,1)}, u32[]{:S(2)}) %copy-start.5) | copy-done | bytes 24600
  4.5 0.0 copy-start.6
  4.5 0.7 %copy-done.6 = s32[16,1,32]{2,1,0:T(1,128)S(1)} copy-done((s32[16,1,32]{2,1,0:T(1,128)S(1)}, s32[16,1,32]{2,1,0:T(1,128)}, u32[]{:S(2)}) %copy-start.6) | copy-done | bytes 2072
  5.2 0.0 copy-start.1
  5.2 41.2 %splat_step.1 = (f32[96,128]{1,0:T(8,128)S(1)}, f32[2,8,1024]{2,1,0:T(8,128)S(1)}) custom-call(f32[53,1024]{1,0:T(8,128)S(1)} %copy-done, f32[2,2,4]{2,1,0:T(2,128)S(1)} %copy-done.7, bf16[3,16,256]{2,1,0:T(8,128)(2,1)S(1)} %bitcast.14, s32[16,512]{1,0:T(8,128)S(1)} %bitcast.12, s32[1,512]{1,0:T(1,128)S(1)} %bitcast.15, s32[32,2,32]{2,1,0:T(2,128)S(1)} %bitcast.13, ...), custom_call_target="tpu_custom_call" | custom-call | tf_op jit(solution)/shard_map/splat_step/pallas_call | solution.py:585
  46.4 0.0 copy-done.1
  46.4 0.0 copy-start.2
  46.4 0.9 %copy-done.2 = f32[53,1024]{1,0:T(8,128)S(1)} copy-done((f32[53,1024]{1,0:T(8,128)S(1)}, f32[53,1024]{1,0:T(8,128)}, u32[]{:S(2)}) %copy-start.2) | copy-done | bytes 217112
  47.3 2.4 %adam.1 = (f32[53,1024]{1,0:T(8,128)}, f32[53,1024]{1,0:T(8,128)}, f32[53,1024]{1,0:T(8,128)}) custom-call(f32[2,8,1024]{2,1,0:T(8,128)S(1)} %get-tuple-element.10.grad_ref, f32[2,2,4]{2,1,0:T(2,128)S(1)} %copy-done.7, f32[53,1024]{1,0:T(8,128)S(1)} %copy-done, f32[53,1024]{1,0:T(8,128)S(1)} %copy-done.1, f32[53,1024]{1,0:T(8,128)S(1)} %copy-done.2), custom_call_target="tpu_custom_call" | custom-call | tf_op jit(solution)/shard_map/adam/pallas_call | solution.py:639
  49.8 0.6 %copy.16 = f32[16,1,3,256]{3,1,2,0:T(1,128)} copy(f32[16,1,3,256]{3,1,2,0:T(1,128)S(1)} %bitcast.11) | data formatting | bytes 98304
Async XLA Ops:
  0.6 0.7 %copy-start.8 = (s32[1,512,1]{1,2,0:T(1,128)S(1)}, s32[1,512,1]{1,2,0:T(1,128)}, u32[]{:S(2)}) copy-start(s32[1,512,1]{1,2,0:T(1,128)} %param.15) | copy-start | bytes 6148
  0.6 0.7 %copy-start.7 = (f32[2,2,4]{2,1,0:T(2,128)S(1)}, f32[2,2,4]{2,1,0:T(2,128)}, u32[]{:S(2)}) copy-start(f32[2,2,4]{2,1,0:T(2,128)} %cam_ref.3) | copy-start | bytes 196
  1.3 0.9 %copy-start = (f32[53,1024]{1,0:T(8,128)S(1)}, f32[53,1024]{1,0:T(8,128)}, u32[]{:S(2)}) copy-start(f32[53,1024]{1,0:T(8,128)} %g_ref.3) | copy-start | bytes 651268
  2.3 0.8 %copy-start.3 = (s32[1,512,1,16]{1,3,2,0:T(8,128)S(1)}, s32[1,512,1,16]{1,3,2,0:T(8,128)}, u32[]{:S(2)}) copy-start(s32[1,512,1,16]{1,3,2,0:T(8,128)} %param.14) | copy-start | bytes 98308
  3.0 0.8 %copy-start.4 = (s32[32,32,1,2]{1,3,2,0:T(2,128)S(1)}, s32[32,32,1,2]{1,3,2,0:T(2,128)}, u32[]{:S(2)}) copy-start(s32[32,32,1,2]{1,3,2,0:T(2,128)} %param.16) | copy-start | bytes 24580
  3.8 0.7 %copy-start.5 = (bf16[16,1,3,256]{3,0,2,1:T(8,128)(2,1)S(1)}, bf16[16,1,3,256]{3,0,2,1:T(8,128)(2,1)}, u32[]{:S(2)}) copy-start(bf16[16,1,3,256]{3,0,2,1:T(8,128)(2,1)} %param.13) | copy-start | bytes 73732
  4.5 0.7 %copy-start.6 = (s32[16,1,32]{2,1,0:T(1,128)S(1)}, s32[16,1,32]{2,1,0:T(1,128)}, u32[]{:S(2)}) copy-start(s32[16,1,32]{2,1,0:T(1,128)} %ord_ref.1) | copy-start | bytes 6148
  5.2 41.2 %copy-start.1 = (f32[53,1024]{1,0:T(8,128)S(1)}, f32[53,1024]{1,0:T(8,128)}, u32[]{:S(2)}) copy-start(f32[53,1024]{1,0:T(8,128)} %one_ref.1) | copy-start | bytes 651268
  46.4 0.9 %copy-start.2 = (f32[53,1024]{1,0:T(8,128)S(1)}, f32[53,1024]{1,0:T(8,128)}, u32[]{:S(2)}) copy-start(f32[53,1024]{1,0:T(8,128)} %two_ref.1) | copy-start | bytes 651268

commit v2 on v1

--- a/solution.py
+++ b/solution.py
@@ -95,6 +95,11 @@
     return high, mid, low
 
 
+def split2(x):
+    high = x.astype(BF16)
+    return high, (x - high.astype(F32)).astype(BF16)
+
+
 def dot(a, b, dims=((1,), (0,))):
     return lax.dot_general(a, b, (dims, ((), ())), preferred_element_type=F32)
 
@@ -110,15 +115,27 @@
 
 
 def step_kernel(
+    g_hbm,
+    one_hbm,
+    two_hbm,
+    cam_hbm,
+    tgt_hbm,
+    ids_hbm,
+    cnt_hbm,
+    isl_hbm,
+    ord_hbm,
+    rend_ref,
+    gout_ref,
+    basis_ref,
+    cam_ref,
     g_ref,
-    cam_ref,
+    one_ref,
+    two_ref,
     tgt_ref,
     ids_ref,
     cnt_ref,
     isl_ref,
     ord_ref,
-    rend_ref,
-    gout_ref,
     tab_send,
     tab_recv,
     fwd_send,
@@ -143,18 +160,35 @@
     lhs_ref,
     sem_ts,
     sem_tr,
-    sem_fs,
-    sem_fr,
-    sem_bs,
-    sem_br,
+    sem_f,
+    sem_b,
     sem_gs,
     sem_gr,
+    sem_in,
 ):
+    loads = [
+        pltpu.make_async_copy(source, target, sem_in.at[at])
+        for at, (source, target) in enumerate(
+            (
+                (g_hbm, g_ref),
+                (cam_hbm, cam_ref),
+                (isl_hbm, isl_ref),
+                (ids_hbm, ids_ref),
+                (cnt_hbm, cnt_ref),
+                (ord_hbm, ord_ref),
+                (tgt_hbm, tgt_ref),
+                (one_hbm, one_ref),
+                (two_hbm, two_ref),
+            )
+        )
+    ]
+    for load in loads[:7]:
+        load.start()
     me_c = lax.axis_index("cell")
     me_v = lax.axis_index("view")
 
     def peer_c(d):
-        return lax.rem(me_c + d, CELLS)
+        return lax.rem(me_c + lax.rem(d + 10, CELLS - 1) + 1, CELLS)
 
     def peer_v(d):
         return lax.rem(me_v + d, VIEWS)
@@ -173,8 +207,12 @@
         )
         return carry
 
+    lax.fori_loop(1, CELLS, greet_cell, 0)
     lax.fori_loop(1, VIEWS, greet_view, 0)
-    lax.fori_loop(1, CELLS, greet_cell, 0)
+    for load in loads[:7]:
+        load.wait()
+    for load in loads[7:]:
+        load.start()
 
     centre = [g_ref[k : k + 1, :] for k in range(3)]
     inv_var = jnp.exp(-2.0 * g_ref[3:4, :])
@@ -182,6 +220,7 @@
     for which in range(2):
         camera = camera_values(cam_ref, which)
         column = basis_column(camera)
+        basis_ref[which] = jnp.broadcast_to(column, (16, LANES))
         screen = [
             row[0] * centre[0] + row[1] * centre[1] + row[2] * centre[2] + row[3] for row in camera
         ]
@@ -194,26 +233,6 @@
         )
         table = jnp.clip(table, -LARGE, LARGE)
         tab_send[which] = jnp.where(table == table, table, 0.0)
-
-    pl.semaphore_wait(barrier, VIEWS - 1 + CELLS - 1)
-
-    def table_copy(d):
-        to = peer_v(d)
-        return pltpu.make_async_remote_copy(
-            src_ref=tab_send.at[to // HALF_VIEWS],
-            dst_ref=tab_recv.at[me_v],
-            send_sem=sem_ts.at[d],
-            recv_sem=sem_tr.at[me_v],
-            device_id=(me_c, to),
-            device_id_type=pl.DeviceIdType.MESH,
-        )
-
-    def table_start(d, carry):
-        table_copy(d).start()
-        return carry
-
-    lax.fori_loop(1, VIEWS, table_start, 0)
-    tab_recv[me_v] = tab_send[me_v // HALF_VIEWS]
 
     lane = iota((1, LANES), 1)
     mine = isl_ref[me_c]
@@ -242,6 +261,56 @@
         for part in range(3):
             oh_ref[part * LANES : (part + 1) * LANES, kk * LANES : (kk + 1) * LANES] = hot
 
+    both = jnp.concatenate([isl_ref[:, 0, :], isl_ref[:, 1, :]], axis=0).astype(F32)
+    at_me = jnp.where(iota((LISTS, CELLS), 1) == me_c, both, 0.0)
+    tile_half = jnp.sum(at_me, axis=1, keepdims=True)
+    tile_col = jnp.concatenate([tile_half, tile_half], axis=0)
+    eye = iota((LANES, LANES), 0) == iota((LANES, LANES), 1)
+    tile_row = jnp.sum(jnp.where(eye, tile_col, 0.0), axis=0, keepdims=True)
+    in_tile = (iota((OWN, LANES), 0).astype(F32) == tile_row).astype(F32)
+    order = ord_ref[...].reshape(OWN, CELLS)
+    cell_lane = lax.rem(iota((OWN, LANES), 1), CELLS)
+    rank = jnp.zeros((OWN, LANES), F32)
+    for at in range(CELLS):
+        rank = jnp.where(order[:, at : at + 1] == cell_lane, float(at), rank)
+    rank_row = jnp.sum(in_tile * rank, axis=0, keepdims=True)
+    key_row = 2.0 * rank_row + jnp.where(lane < LISTS, 0.0, 1.0)
+    key_col = jnp.sum(jnp.where(eye, key_row, 0.0), axis=1, keepdims=True)
+    same = (tile_col == tile_row) & (tile_row >= 0.0)
+    ahead = (same & (key_col < key_row)).astype(F32).astype(BF16)
+    after = (same & (key_col > key_row)).astype(F32).astype(BF16)
+    ahead3 = jnp.concatenate([ahead] * 3, axis=0)
+    after2 = jnp.concatenate([after] * 2, axis=0)
+    in_tile_b = in_tile.astype(BF16)
+    in_tile3 = jnp.concatenate([in_tile_b] * 3, axis=1)
+    in_tile2v = jnp.concatenate([in_tile_b] * 2, axis=0)
+    tile_int = tile_row.astype(jnp.int32)
+    window = lax.rem(me_v, HALF_VIEWS) * ROWS + me_c * OWN + tile_int
+    side_at = iota((TSIDE, LANES), 0).astype(F32) + 0.5
+    place_x = (lax.rem(window, 32) * TSIDE).astype(F32) + side_at
+    place_y = ((window // 32) * TSIDE).astype(F32) + side_at
+    acc_ref[...] = jnp.zeros_like(acc_ref)
+
+    pl.semaphore_wait(barrier, VIEWS - 1 + CELLS - 1)
+
+    def table_copy(d):
+        to = peer_v(d)
+        return pltpu.make_async_remote_copy(
+            src_ref=tab_send.at[to // HALF_VIEWS],
+            dst_ref=tab_recv.at[me_v],
+            send_sem=sem_ts.at[d],
+            recv_sem=sem_tr.at[me_v],
+            device_id=(me_c, to),
+            device_id_type=pl.DeviceIdType.MESH,
+        )
+
+    def table_start(d, carry):
+        table_copy(d).start()
+        return carry
+
+    lax.fori_loop(1, VIEWS, table_start, 0)
+    tab_recv[me_v] = tab_send[me_v // HALF_VIEWS]
+
     def table_wait(d, carry):
         pltpu.make_async_remote_copy(
             src_ref=tab_send.at[0],
@@ -277,68 +346,28 @@
     fwd_send[:, 0, :] = lists[:CELLS]
     fwd_send[:, 1, :] = lists[CELLS:]
 
-    def cell_copy(source, target, send, recv, d):
+    def cell_copy(source, target, sems, d):
         return pltpu.make_async_remote_copy(
             src_ref=source.at[peer_c(d)],
             dst_ref=target.at[me_c],
-            send_sem=send.at[d],
-            recv_sem=recv.at[me_c],
+            send_sem=sems.at[0],
+            recv_sem=sems.at[1],
             device_id=(peer_c(d), me_v),
             device_id_type=pl.DeviceIdType.MESH,
         )
 
-    def cell_arrived(source, target, send, recv, d):
-        return pltpu.make_async_remote_copy(
-            src_ref=source.at[peer_c(d)],
-            dst_ref=target.at[peer_c(d)],
-            send_sem=send.at[d],
-            recv_sem=recv.at[peer_c(d)],
-            device_id=(peer_c(d), me_v),
-            device_id_type=pl.DeviceIdType.MESH,
-        )
+    def cell_wait(buffer, sem):
+        others = buffer.at[pl.ds(0, CELLS - 1)]
+        pltpu.make_async_copy(others, others, sem).wait()
 
     def fwd_start(d, carry):
-        cell_copy(fwd_send, fwd_recv, sem_fs, sem_fr, d).start()
+        cell_copy(fwd_send, fwd_recv, sem_f, d).start()
         return carry
 
     lax.fori_loop(1, CELLS, fwd_start, 0)
     fwd_recv[me_c] = fwd_send[me_c]
 
-    both = jnp.concatenate([isl_ref[:, 0, :], isl_ref[:, 1, :]], axis=0).astype(F32)
-    at_me = jnp.where(iota((LISTS, CELLS), 1) == me_c, both, 0.0)
-    tile_half = jnp.sum(at_me, axis=1, keepdims=True)
-    tile_col = jnp.concatenate([tile_half, tile_half], axis=0)
-    eye = iota((LANES, LANES), 0) == iota((LANES, LANES), 1)
-    tile_row = jnp.sum(jnp.where(eye, tile_col, 0.0), axis=0, keepdims=True)
-    in_tile = (iota((OWN, LANES), 0).astype(F32) == tile_row).astype(F32)
-    order = ord_ref[...].reshape(OWN, CELLS)
-    cell_lane = lax.rem(iota((OWN, LANES), 1), CELLS)
-    rank = jnp.zeros((OWN, LANES), F32)
-    for at in range(CELLS):
-        rank = jnp.where(order[:, at : at + 1] == cell_lane, float(at), rank)
-    rank_row = jnp.sum(in_tile * rank, axis=0, keepdims=True)
-    key_row = 2.0 * rank_row + jnp.where(lane < LISTS, 0.0, 1.0)
-    key_col = jnp.sum(jnp.where(eye, key_row, 0.0), axis=1, keepdims=True)
-    same = (tile_col == tile_row) & (tile_row >= 0.0)
-    ahead = (same & (key_col < key_row)).astype(F32).astype(BF16)
-    after = (same & (key_col > key_row)).astype(F32).astype(BF16)
-    ahead3 = jnp.concatenate([ahead] * 3, axis=0)
-    after3 = jnp.concatenate([after] * 3, axis=0)
-    in_tile_b = in_tile.astype(BF16)
-    in_tile3 = jnp.concatenate([in_tile_b] * 3, axis=1)
-    in_tile3v = jnp.concatenate([in_tile_b] * 3, axis=0)
-    tile_int = tile_row.astype(jnp.int32)
-    window = lax.rem(me_v, HALF_VIEWS) * ROWS + me_c * OWN + tile_int
-    side_at = iota((TSIDE, LANES), 0).astype(F32) + 0.5
-    place_x = (lax.rem(window, 32) * TSIDE).astype(F32) + side_at
-    place_y = ((window // 32) * TSIDE).astype(F32) + side_at
-    acc_ref[...] = jnp.zeros_like(acc_ref)
-
-    def fwd_wait(d, carry):
-        cell_arrived(fwd_send, fwd_recv, sem_fs, sem_fr, d).wait_recv()
-        return carry
-
-    lax.fori_loop(1, CELLS, fwd_wait, 0)
+    cell_wait(fwd_recv, sem_f.at[1])
     v_ref[...] = lists_to_rows(
         jnp.concatenate([fwd_recv[:, 0, :], fwd_recv[:, 1, :]], axis=0)
     )
@@ -392,11 +421,11 @@
         rend_ref[pl.ds(2 * ch, OWN, stride=6), :] = image[:, :LANES]
         rend_ref[pl.ds(2 * ch + 1, OWN, stride=6), :] = image[:, LANES:]
         miss = image - tgt_ref[ch].astype(F32)
-        miss3 = jnp.concatenate(split3(miss), axis=0)
-        pulled = dot(miss3, in_tile3v, ((0,), (0,)))
+        miss2 = jnp.concatenate(split2(miss), axis=0)
+        pulled = dot(miss2, in_tile2v, ((0,), (0,)))
         gl_ref[ch] = pulled
         owed = owed + seen * pulled
-    behind_ref[...] = dot(jnp.concatenate(split3(owed), axis=1), after3)
+    behind_ref[...] = dot(jnp.concatenate(split2(owed), axis=1), after2)
 
     def backward(i, carry):
         rows = pl.ds(pl.multiple_of(i * 32, 32), 32)
@@ -451,27 +480,23 @@
     bwd_send[:, 1, :] = lists[CELLS:]
 
     def bwd_start(d, carry):
-        cell_copy(bwd_send, bwd_recv, sem_bs, sem_br, d).start()
+        cell_copy(bwd_send, bwd_recv, sem_b, d).start()
         return carry
 
     lax.fori_loop(1, CELLS, bwd_start, 0)
     bwd_recv[me_c] = bwd_send[me_c]
 
-    def bwd_wait(d, carry):
-        cell_arrived(bwd_send, bwd_recv, sem_bs, sem_br, d).wait_recv()
-        return carry
-
-    lax.fori_loop(1, CELLS, bwd_wait, 0)
+    cell_wait(bwd_recv, sem_b.at[1])
 
     grads = lists_to_rows(jnp.concatenate([bwd_recv[:, 0, :], bwd_recv[:, 1, :]], axis=0))
     last = iota((SUB, LANES), 0) == SUB - 1
     for kk in range(SUB):
         hi = hi_ref[kk : kk + 1, :]
-        piece = split3(jnp.where(last, 1.0, grads[kk * SUB : (kk + 1) * SUB]))
+        piece = split2(jnp.where(last, 1.0, grads[kk * SUB : (kk + 1) * SUB]))
         piece = [x.astype(F32) for x in piece]
         for at in range(0, HIGHS, 2):
             here, there = hi == float(at), hi == float(at + 1)
-            for part in range(3):
+            for part in range(2):
                 lhs_ref[part, at * SUB : (at + 2) * SUB, kk * LANES : (kk + 1) * LANES] = (
                     jnp.concatenate(
                         [jnp.where(here, piece[part], 0.0), jnp.where(there, piece[part], 0.0)],
@@ -481,7 +506,6 @@
     hot = oh_ref[0:LANES, :]
     spread = dot(lhs_ref[0], hot, ((1,), (1,)))
     spread = spread + dot(lhs_ref[1], hot, ((1,), (1,)))
-    spread = spread + dot(lhs_ref[2], hot, ((1,), (1,)))
     for home in range(VIEWS):
         for at in range(SUB):
             row = (home * SUB + at) * SUB
@@ -525,48 +549,72 @@
         grad_arrived(d).wait_send()
         return carry
 
-    def sent_cell(d, carry):
-        cell_copy(fwd_send, fwd_recv, sem_fs, sem_fr, d).wait_send()
-        cell_copy(bwd_send, bwd_recv, sem_bs, sem_br, d).wait_send()
-        return carry
-
+    for load in loads[7:]:
+        load.wait()
     lax.fori_loop(1, VIEWS, sent_view, 0)
-    lax.fori_loop(1, CELLS, sent_cell, 0)
-
-
-def adam_kernel(grad_ref, cam_ref, g_ref, one_ref, two_ref, new_g, new_one, new_two):
+    cell_wait(fwd_send, sem_f.at[0])
+    cell_wait(bwd_send, sem_b.at[0])
+
+
+def adam_kernel(
+    grad_ref,
+    rend_ref,
+    basis_ref,
+    cam_ref,
+    g_ref,
+    one_ref,
+    two_ref,
+    rend_out,
+    out_g,
+    out_one,
+    out_two,
+    grads,
+    new_g,
+    new_one,
+    new_two,
+    sems,
+):
+    image = pltpu.make_async_copy(rend_ref, rend_out, sems.at[0, 0])
+    image.start()
     touched = grad_ref[0, 7:8, :] + grad_ref[1, 7:8, :] > 0.5
     cameras = [camera_values(cam_ref, which) for which in range(2)]
-    columns = [basis_column(camera) for camera in cameras]
     fix_one = 1.0 / (1.0 - beta_one**adam_step)
     fix_two = 1.0 / (1.0 - beta_two**adam_step)
-
-    def update(rows, grad):
+    for k in range(3):
+        grads[k : k + 1, :] = sum(
+            cameras[which][row][k] * grad_ref[which, row : row + 1, :]
+            for which in range(2)
+            for row in range(2)
+        )
+    grads[3:5, :] = grad_ref[0, 2:4, :] + grad_ref[1, 2:4, :]
+    columns = [basis_ref[which, :, 0:1] for which in range(2)]
+    for ch in range(3):
+        j = 4 + ch
+        grads[5 + 16 * ch : 21 + 16 * ch, :] = (
+            columns[0] * grad_ref[0, j : j + 1, :] + columns[1] * grad_ref[1, j : j + 1, :]
+        )
+    copies = [image]
+    for at, (low, high) in enumerate(((0, 16), (16, 32), (32, 48), (48, 53))):
+        rows = slice(low, high)
+        grad = grads[rows, :]
         first = beta_one * one_ref[rows, :] + (1.0 - beta_one) * grad
         second = beta_two * two_ref[rows, :] + (1.0 - beta_two) * grad * grad
         change = learn_rate * (first * fix_one) / (jnp.sqrt(second * fix_two) + adam_eps)
         new_g[rows, :] = jnp.where(touched, g_ref[rows, :] - change, g_ref[rows, :])
         new_one[rows, :] = jnp.where(touched, first, one_ref[rows, :])
         new_two[rows, :] = jnp.where(touched, second, two_ref[rows, :])
-
-    small = []
-    for k in range(3):
-        small.append(
-            sum(
-                cameras[which][row][k] * grad_ref[which, row : row + 1, :]
-                for which in range(2)
-                for row in range(2)
+        for which, (source, target) in enumerate(
+            ((new_g, out_g), (new_one, out_one), (new_two, out_two))
+        ):
+            copy = pltpu.make_async_copy(
+                source.at[pl.ds(low, high - low), :],
+                target.at[pl.ds(low, high - low), :],
+                sems.at[1 + at, which],
             )
-        )
-    for j in (2, 3):
-        small.append(grad_ref[0, j : j + 1, :] + grad_ref[1, j : j + 1, :])
-    update(slice(0, 5), jnp.concatenate(small, axis=0))
-    for ch in range(3):
-        j = 4 + ch
-        update(
-            slice(5 + 16 * ch, 21 + 16 * ch),
-            columns[0] * grad_ref[0, j : j + 1, :] + columns[1] * grad_ref[1, j : j + 1, :],
-        )
+            copy.start()
+            copies.append(copy)
+    for copy in copies:
+        copy.wait()
 
 
 def per_device(
@@ -581,16 +629,28 @@
     depth_order,
 ):
     vmem = pl.BlockSpec(memory_space=pltpu.VMEM)
+    hbm = pl.BlockSpec(memory_space=pltpu.HBM)
+    shape = jax.ShapeDtypeStruct(gaussians.shape, F32)
     sems = pltpu.SemaphoreType.DMA
-    rendered, grads = pl.pallas_call(
+    rendered, grads, basis, cameras, gaussians, moment_one, moment_two = pl.pallas_call(
         step_kernel,
         out_shape=(
             jax.ShapeDtypeStruct((96, LANES), F32),
             jax.ShapeDtypeStruct((2, SUB, HOME), F32),
+            jax.ShapeDtypeStruct((2, 16, LANES), F32),
+            jax.ShapeDtypeStruct((2, 2, 4), F32),
+            shape,
+            shape,
+            shape,
         ),
-        in_specs=[vmem] * 7,
-        out_specs=(vmem, vmem),
+        in_specs=[hbm] * 9,
+        out_specs=(vmem,) * 7,
         scratch_shapes=[
+            pltpu.VMEM((3, OWN, PIX), BF16),
+            pltpu.VMEM((16, ROWS), jnp.int32),
+            pltpu.VMEM((1, ROWS), jnp.int32),
+            pltpu.VMEM((CELLS, 2, CELLS), jnp.int32),
+            pltpu.VMEM((OWN, 1, CELLS), jnp.int32),
             pltpu.VMEM((2, SUB, HOME), F32),
             pltpu.VMEM((VIEWS, SUB, HOME), F32),
             pltpu.VMEM((CELLS, 2, LANES), F32),
@@ -612,39 +672,51 @@
             pltpu.VMEM((PIX, LANES), F32),
             pltpu.VMEM((3, PIX, LANES), F32),
             pltpu.VMEM((SUB, 6, TSIDE, LANES), F32),
-            pltpu.VMEM((3, HIGHS * SUB, SUB * LANES), BF16),
+            pltpu.VMEM((2, HIGHS * SUB, SUB * LANES), BF16),
             sems((VIEWS,)),
             sems((VIEWS,)),
-            sems((CELLS,)),
-            sems((CELLS,)),
-            sems((CELLS,)),
-            sems((CELLS,)),
+            sems((2,)),
+            sems((2,)),
             sems((VIEWS,)),
             sems((VIEWS,)),
+            sems((9,)),
         ],
         compiler_params=pltpu.CompilerParams(
             collective_id=0, has_side_effects=True, vmem_limit_bytes=40 * 1024 * 1024
         ),
         name="splat_step",
     )(
-        gaussians,
-        cameras,
-        jnp.transpose(target[:, 0], (1, 0, 2)),
-        jnp.transpose(gauss_ids[0, :, 0, :], (1, 0)),
-        tile_counts.reshape(1, ROWS),
-        jnp.transpose(intersection_slots[:, :, 0, :], (0, 2, 1)),
-        depth_order,
+        *(
+            pltpu.with_memory_space_constraint(x, pltpu.HBM)
+            for x in (
+                gaussians,
+                moment_one,
+                moment_two,
+                cameras,
+                jnp.transpose(target[:, 0], (1, 0, 2)),
+                jnp.transpose(gauss_ids[0, :, 0, :], (1, 0)),
+                tile_counts.reshape(1, ROWS),
+                jnp.transpose(intersection_slots[:, :, 0, :], (0, 2, 1)),
+                depth_order,
+            )
+        )
     )
-    shape = jax.ShapeDtypeStruct(gaussians.shape, F32)
-    new_gaussians, new_one, new_two = pl.pallas_call(
+    image, new_gaussians, new_one, new_two = pl.pallas_call(
         adam_kernel,
-        out_shape=(shape, shape, shape),
-        in_specs=[vmem] * 5,
-        out_specs=(vmem,) * 3,
+        out_shape=(jax.ShapeDtypeStruct((96, LANES), F32), shape, shape, shape),
+        in_specs=[vmem] * 7,
+        out_specs=(hbm,) * 4,
+        scratch_shapes=[
+            pltpu.VMEM((56, HOME), F32),
+            pltpu.VMEM(gaussians.shape, F32),
+            pltpu.VMEM(gaussians.shape, F32),
+            pltpu.VMEM(gaussians.shape, F32),
+            sems((5, 3)),
+        ],
         compiler_params=pltpu.CompilerParams(vmem_limit_bytes=20 * 1024 * 1024),
         name="adam",
-    )(grads, cameras, gaussians, moment_one, moment_two)
-    return (rendered.reshape(OWN, 1, 3, PIX), new_gaussians, new_one, new_two)
+    )(grads, rendered, basis, cameras, gaussians, moment_one, moment_two)
+    return (image.reshape(OWN, 1, 3, PIX), new_gaussians, new_one, new_two)
 
 
 def solution(mesh):

time: 50.8 us -> 41.6 us (0.82)
  local copies, waits for them, and re-layouts: 6.13 us -> 0 us
  Pallas kernels: 43.6 us -> 40.8 us
    unnamed x19 -> x0, local copies, waits for them, and re-layouts: 6.13 us -> none
    pallas_call x1, Pallas kernels: 41.2 us -> 39.7 us  [per_device(): pl.pallas_call(step_kernel, out_shape=(jax.ShapeDtypeStruct((96, LANES),...]
    pallas_call x1, Pallas kernels: 2.4 us -> 1.2 us  [per_device(): pl.pallas_call(adam_kernel, out_shape=(jax.ShapeDtypeStruct((96, LANES),...]
where the time goes in v2:
time: 41.6 us; the launch traced here: 41.5 us
  Pallas kernels  40.8 us (98%)
  between operations  0.64 us (2%)
    pallas_call x1, Pallas kernels, per_device(): pl.pallas_call(step_kernel, out_shape=(jax.ShapeDtypeStruct((96, LANES),...  39.7 us
    pallas_call x1, Pallas kernels, per_device(): pl.pallas_call(adam_kernel, out_shape=(jax.ShapeDtypeStruct((96, LANES),...  1.2 us

profile of v2, /device:TPU:1, one launch (start us, length us, event | category | flops | bytes accessed | tf_op | source)
XLA Modules:
  0.0 41.5 jit_solution(12040649536450004582)
XLA Ops:
  0.6 39.7 %splat_step.1 = (f32[96,128]{1,0:T(8,128)S(1)}, f32[2,8,1024]{2,1,0:T(8,128)S(1)}, f32[2,16,128]{2,1,0:T(8,128)S(1)}, f32[2,2,4]{2,1,0:T(2,128)S(1)}, f32[53,102...) custom-call(f32[53,1024]{1,0:T(8,128)} %g_hbm.1, f32[53,1024]{1,0:T(8,128)} %one_hbm.1, ...), custom_call_target="tpu_custom_call" | custom-call | tf_op jit(solution)/shard_map/splat_step/pallas_call | solution.py:635
  40.3 1.2 %adam.1 = (f32[96,128]{1,0:T(8,128)}, f32[53,1024]{1,0:T(8,128)}, f32[53,1024]{1,0:T(8,128)}, f32[53,1024]{1,0:T(8,128)}) custom-call(f32[2,8,1024]{2,1,0:T(8,128)S(1)} %get-tuple-element.15.grad_ref, f32[96,128]{1,0:T(8,128)S(1)} %get-tuple-element.16.rend_ref, f32[2,16,128]{2,1,0:T(8,128)S(1)} %get-tuple-element.17.basis_ref, ...), custom_call_target="tpu_custom_call" | custom-call | tf_op jit(solution)/shard_map/adam/pallas_call | solution.py:704

commit v3 on v2

--- a/solution.py
+++ b/solution.py
@@ -165,6 +165,8 @@
     sem_gs,
     sem_gr,
     sem_in,
+    near_sem,
+    line_sem,
 ):
     loads = [
         pltpu.make_async_copy(source, target, sem_in.at[at])
@@ -190,25 +192,48 @@
     def peer_c(d):
         return lax.rem(me_c + lax.rem(d + 10, CELLS - 1) + 1, CELLS)
 
-    def peer_v(d):
-        return lax.rem(me_v + d, VIEWS)
+    me_x, me_core = me_v // 2, lax.rem(me_v, 2)
+    me_y, me_z = me_c // 8, lax.rem(me_c, 8)
+
+    def chip_v(step):
+        return 2 * lax.rem(me_x + step, 4)
+
+    peers_v = [chip_v(step) + core for step in (2, 1, 3) for core in range(2)]
+    peers_v.append(me_v + 1 - 2 * me_core)
+
+    def near_z(d):
+        return me_y * 8 + lax.rem(me_z + d + 1 + 3 * (d // 2), 8)
+
+    def line_y(d):
+        return lax.rem(me_y + d, 4) * 8 + me_z
+
+    def signal(sem, cell):
+        pl.semaphore_signal(
+            sem, inc=1, device_id=(cell, me_v), device_id_type=pl.DeviceIdType.MESH
+        )
 
     barrier = pltpu.get_barrier_semaphore()
 
-    def greet_cell(d, carry):
+    def greet_z(sem):
+        def body(d, carry):
+            signal(sem, near_z(d))
+            return carry
+
+        lax.fori_loop(0, 4, body, 0)
+
+    def greet_y(sem):
+        def body(d, carry):
+            signal(sem, line_y(d))
+            return carry
+
+        lax.fori_loop(1, 4, body, 0)
+
+    greet_z(barrier)
+    greet_y(barrier)
+    for peer in peers_v:
         pl.semaphore_signal(
-            barrier, inc=1, device_id=(peer_c(d), me_v), device_id_type=pl.DeviceIdType.MESH
-        )
-        return carry
-
-    def greet_view(d, carry):
-        pl.semaphore_signal(
-            barrier, inc=1, device_id=(me_c, peer_v(d)), device_id_type=pl.DeviceIdType.MESH
-        )
-        return carry
-
-    lax.fori_loop(1, CELLS, greet_cell, 0)
-    lax.fori_loop(1, VIEWS, greet_view, 0)
+            barrier, inc=1, device_id=(me_c, peer), device_id_type=pl.DeviceIdType.MESH
+        )
     for load in loads[:7]:
         load.wait()
     for load in loads[7:]:
@@ -291,57 +316,61 @@
     place_y = ((window // 32) * TSIDE).astype(F32) + side_at
     acc_ref[...] = jnp.zeros_like(acc_ref)
 
-    pl.semaphore_wait(barrier, VIEWS - 1 + CELLS - 1)
-
-    def table_copy(d):
-        to = peer_v(d)
+    pl.semaphore_wait(barrier, VIEWS - 1 + 7)
+    greet_z(near_sem)
+    greet_y(near_sem)
+
+    def table_copy(at):
+        to = peers_v[at]
         return pltpu.make_async_remote_copy(
             src_ref=tab_send.at[to // HALF_VIEWS],
             dst_ref=tab_recv.at[me_v],
-            send_sem=sem_ts.at[d],
+            send_sem=sem_ts.at[at],
             recv_sem=sem_tr.at[me_v],
             device_id=(me_c, to),
             device_id_type=pl.DeviceIdType.MESH,
         )
 
-    def table_start(d, carry):
-        table_copy(d).start()
-        return carry
-
-    lax.fori_loop(1, VIEWS, table_start, 0)
-    tab_recv[me_v] = tab_send[me_v // HALF_VIEWS]
-
-    def table_wait(d, carry):
+    def table_wait(at):
         pltpu.make_async_remote_copy(
             src_ref=tab_send.at[0],
-            dst_ref=tab_recv.at[peer_v(d)],
-            send_sem=sem_ts.at[d],
-            recv_sem=sem_tr.at[peer_v(d)],
-            device_id=(me_c, peer_v(d)),
+            dst_ref=tab_recv.at[peers_v[at]],
+            send_sem=sem_ts.at[at],
+            recv_sem=sem_tr.at[peers_v[at]],
+            device_id=(me_c, peers_v[at]),
             device_id_type=pl.DeviceIdType.MESH,
         ).wait_recv()
-        return carry
-
-    lax.fori_loop(1, VIEWS, table_wait, 0)
-
-    blocks = []
-    for home in range(VIEWS):
-        for at in range(SUB):
-            value = tab_recv[home, :, at * LANES : (at + 1) * LANES]
-            blocks.append(value)
-    parts = split3(jnp.concatenate(blocks, axis=0))
-    lhs = jnp.concatenate(parts, axis=1)
-    chosen = []
-    for pair in range(4):
-        got = dot(lhs, oh_ref[:, pair * 256 : (pair + 1) * 256])
-        for side in range(2):
-            hi = hi_ref[2 * pair + side : 2 * pair + side + 1, :]
-            total = jnp.zeros((SUB, LANES), F32)
-            for at in range(HIGHS):
-                total = total + jnp.where(
-                    hi == float(at), got[at * SUB : (at + 1) * SUB, side * LANES : (side + 1) * LANES], 0.0
-                )
-            chosen.append(total)
+
+    for at in range(VIEWS - 1):
+        table_copy(at).start()
+    tab_recv[me_v] = tab_send[me_v // HALF_VIEWS]
+
+    chosen = [jnp.zeros((SUB, LANES), F32) for kk in range(SUB)]
+    for group, (steps, arrivals) in enumerate((((0,), (6,)), ((1, 3), (2, 3, 4, 5)), ((2,), (0, 1)))):
+        for at in arrivals:
+            table_wait(at)
+        if group == 0:
+            pl.semaphore_wait(near_sem, 7)
+            greet_y(line_sem)
+        blocks, highs = [], []
+        for step in steps:
+            for core in range(2):
+                home = chip_v(step) + core
+                for at in range(SUB):
+                    blocks.append(tab_recv[home, :, at * LANES : (at + 1) * LANES])
+                    highs.append((home * SUB + at).astype(F32))
+        lhs = jnp.concatenate(split3(jnp.concatenate(blocks, axis=0)), axis=1)
+        for pair in range(4):
+            got = dot(lhs, oh_ref[:, pair * 256 : (pair + 1) * 256])
+            for side in range(2):
+                kk = 2 * pair + side
+                hi = hi_ref[kk : kk + 1, :]
+                for at, value_at in enumerate(highs):
+                    chosen[kk] = chosen[kk] + jnp.where(
+                        hi == value_at,
+                        got[at * SUB : (at + 1) * SUB, side * LANES : (side + 1) * LANES],
+                        0.0,
+                    )
     lists = rows_to_lists(jnp.concatenate(chosen, axis=0))
     fwd_send[:, 0, :] = lists[:CELLS]
     fwd_send[:, 1, :] = lists[CELLS:]
@@ -364,6 +393,7 @@
         cell_copy(fwd_send, fwd_recv, sem_f, d).start()
         return carry
 
+    pl.semaphore_wait(line_sem, 3)
     lax.fori_loop(1, CELLS, fwd_start, 0)
     fwd_recv[me_c] = fwd_send[me_c]
 
@@ -490,68 +520,70 @@
 
     grads = lists_to_rows(jnp.concatenate([bwd_recv[:, 0, :], bwd_recv[:, 1, :]], axis=0))
     last = iota((SUB, LANES), 0) == SUB - 1
+    pieces = []
     for kk in range(SUB):
-        hi = hi_ref[kk : kk + 1, :]
         piece = split2(jnp.where(last, 1.0, grads[kk * SUB : (kk + 1) * SUB]))
-        piece = [x.astype(F32) for x in piece]
-        for at in range(0, HIGHS, 2):
-            here, there = hi == float(at), hi == float(at + 1)
-            for part in range(2):
-                lhs_ref[part, at * SUB : (at + 2) * SUB, kk * LANES : (kk + 1) * LANES] = (
-                    jnp.concatenate(
-                        [jnp.where(here, piece[part], 0.0), jnp.where(there, piece[part], 0.0)],
-                        axis=0,
-                    ).astype(BF16)
-                )
+        pieces.append([x.astype(F32) for x in piece])
     hot = oh_ref[0:LANES, :]
-    spread = dot(lhs_ref[0], hot, ((1,), (1,)))
-    spread = spread + dot(lhs_ref[1], hot, ((1,), (1,)))
-    for home in range(VIEWS):
-        for at in range(SUB):
-            row = (home * SUB + at) * SUB
-            grad_send[home, :, at * LANES : (at + 1) * LANES] = spread[row : row + SUB]
-
-    def grad_start(d, carry):
-        to = peer_v(d)
-        pltpu.make_async_remote_copy(
-            src_ref=grad_send.at[to],
+
+    def grad_copy(at):
+        return pltpu.make_async_remote_copy(
+            src_ref=grad_send.at[peers_v[at]],
             dst_ref=grad_recv.at[me_v],
-            send_sem=sem_gs.at[d],
+            send_sem=sem_gs.at[at],
             recv_sem=sem_gr.at[me_v],
-            device_id=(me_c, to),
+            device_id=(me_c, peers_v[at]),
             device_id_type=pl.DeviceIdType.MESH,
-        ).start()
-        return carry
-
-    lax.fori_loop(1, VIEWS, grad_start, 0)
+        )
+
+    def grad_arrived(at):
+        return pltpu.make_async_remote_copy(
+            src_ref=grad_send.at[peers_v[at]],
+            dst_ref=grad_recv.at[peers_v[at]],
+            send_sem=sem_gs.at[at],
+            recv_sem=sem_gr.at[peers_v[at]],
+            device_id=(me_c, peers_v[at]),
+            device_id_type=pl.DeviceIdType.MESH,
+        )
+
+    for steps, sends in (((2,), (0, 1)), ((1, 3), (2, 3, 4, 5)), ((0,), (6,))):
+        homes = [chip_v(step) + core for step in steps for core in range(2)]
+        count = len(homes) * SUB
+        for kk in range(SUB):
+            hi = hi_ref[kk : kk + 1, :]
+            for at in range(0, count, 2):
+                first = (homes[at // SUB] * SUB + at % SUB).astype(F32)
+                here, there = hi == first, hi == first + 1.0
+                for part in range(2):
+                    lhs_ref[part, at * SUB : (at + 2) * SUB, kk * LANES : (kk + 1) * LANES] = (
+                        jnp.concatenate(
+                            [
+                                jnp.where(here, pieces[kk][part], 0.0),
+                                jnp.where(there, pieces[kk][part], 0.0),
+                            ],
+                            axis=0,
+                        ).astype(BF16)
+                    )
+        rows = slice(0, count * SUB)
+        spread = dot(lhs_ref[0, rows, :], hot, ((1,), (1,)))
+        spread = spread + dot(lhs_ref[1, rows, :], hot, ((1,), (1,)))
+        for which, home in enumerate(homes):
+            for at in range(SUB):
+                row = (which * SUB + at) * SUB
+                grad_send[home, :, at * LANES : (at + 1) * LANES] = spread[row : row + SUB]
+        for at in sends:
+            grad_copy(at).start()
     grad_recv[me_v] = grad_send[me_v]
-
-    def grad_arrived(d):
-        return pltpu.make_async_remote_copy(
-            src_ref=grad_send.at[peer_v(d)],
-            dst_ref=grad_recv.at[peer_v(d)],
-            send_sem=sem_gs.at[d],
-            recv_sem=sem_gr.at[peer_v(d)],
-            device_id=(me_c, peer_v(d)),
-            device_id_type=pl.DeviceIdType.MESH,
-        )
-
-    def grad_wait(d, carry):
-        grad_arrived(d).wait_recv()
-        return carry
-
-    lax.fori_loop(1, VIEWS, grad_wait, 0)
+    for at in range(VIEWS - 1):
+        grad_arrived(at).wait_recv()
     gout_ref[0] = (grad_recv[0] + grad_recv[1]) + (grad_recv[2] + grad_recv[3])
     gout_ref[1] = (grad_recv[4] + grad_recv[5]) + (grad_recv[6] + grad_recv[7])
 
-    def sent_view(d, carry):
-        table_copy(d).wait_send()
-        grad_arrived(d).wait_send()
-        return carry
-
     for load in loads[7:]:
         load.wait()
-    lax.fori_loop(1, VIEWS, sent_view, 0)
+    for at in range(VIEWS - 1):
+        table_copy(at).wait_send()
+        grad_copy(at).wait_send()
     cell_wait(fwd_send, sem_f.at[0])
     cell_wait(bwd_send, sem_b.at[0])
 
@@ -672,7 +704,7 @@
             pltpu.VMEM((PIX, LANES), F32),
             pltpu.VMEM((3, PIX, LANES), F32),
             pltpu.VMEM((SUB, 6, TSIDE, LANES), F32),
-            pltpu.VMEM((2, HIGHS * SUB, SUB * LANES), BF16),
+            pltpu.VMEM((2, HIGHS * SUB // 2, SUB * LANES), BF16),
             sems((VIEWS,)),
             sems((VIEWS,)),
             sems((2,)),
@@ -680,6 +712,8 @@
             sems((VIEWS,)),
             sems((VIEWS,)),
             sems((9,)),
+            pltpu.SemaphoreType.REGULAR,
+            pltpu.SemaphoreType.REGULAR,
         ],
         compiler_params=pltpu.CompilerParams(
             collective_id=0, has_side_effects=True, vmem_limit_bytes=40 * 1024 * 1024

time: 41.6 us -> 37.5 us (0.901)
  Pallas kernels: 40.8 us -> 36.8 us
    pallas_call x1, Pallas kernels: 39.7 us -> 35.6 us  [per_device(): pl.pallas_call(step_kernel, out_shape=(jax.ShapeDtypeStruct((96, LANES),...]
where the time goes in v3:
time: 37.5 us; the launch traced here: 37.4 us
  Pallas kernels  36.8 us (98%)
  between operations  0.64 us (2%)
    pallas_call x1, Pallas kernels, per_device(): pl.pallas_call(step_kernel, out_shape=(jax.ShapeDtypeStruct((96, LANES),...  35.6 us
    pallas_call x1, Pallas kernels, per_device(): pl.pallas_call(adam_kernel, out_shape=(jax.ShapeDtypeStruct((96, LANES),...  1.2 us

profile of v3, /device:TPU:1, one launch (start us, length us, event | category | flops | bytes accessed | tf_op | source)
XLA Modules:
  0.0 37.4 jit_solution(11810494462989195353)
XLA Ops:
  0.6 35.6 %splat_step.1 = (f32[96,128]{1,0:T(8,128)S(1)}, f32[2,8,1024]{2,1,0:T(8,128)S(1)}, f32[2,16,128]{2,1,0:T(8,128)S(1)}, f32[2,2,4]{2,1,0:T(2,128)S(1)}, f32[53,102...) custom-call(f32[53,1024]{1,0:T(8,128)} %g_hbm.1, f32[53,1024]{1,0:T(8,128)} %one_hbm.1, ...), custom_call_target="tpu_custom_call" | custom-call | tf_op jit(solution)/shard_map/splat_step/pallas_call | solution.py:667
  36.2 1.2 %adam.1 = (f32[96,128]{1,0:T(8,128)}, f32[53,1024]{1,0:T(8,128)}, f32[53,1024]{1,0:T(8,128)}, f32[53,1024]{1,0:T(8,128)}) custom-call(f32[2,8,1024]{2,1,0:T(8,128)S(1)} %get-tuple-element.15.grad_ref, f32[96,128]{1,0:T(8,128)S(1)} %get-tuple-element.16.rend_ref, f32[2,16,128]{2,1,0:T(8,128)S(1)} %get-tuple-element.17.basis_ref, ...), custom_call_target="tpu_custom_call" | custom-call | tf_op jit(solution)/shard_map/adam/pallas_call | solution.py:738

commit v4 on v3

--- a/solution.py
+++ b/solution.py
@@ -157,6 +157,7 @@
     behind_ref,
     gl_ref,
     acc_ref,
+    sum_ref,
     lhs_ref,
     sem_ts,
     sem_tr,
@@ -304,10 +305,10 @@
     same = (tile_col == tile_row) & (tile_row >= 0.0)
     ahead = (same & (key_col < key_row)).astype(F32).astype(BF16)
     after = (same & (key_col > key_row)).astype(F32).astype(BF16)
-    ahead3 = jnp.concatenate([ahead] * 3, axis=0)
+    ahead2 = jnp.concatenate([ahead] * 2, axis=0)
     after2 = jnp.concatenate([after] * 2, axis=0)
     in_tile_b = in_tile.astype(BF16)
-    in_tile3 = jnp.concatenate([in_tile_b] * 3, axis=1)
+    in_tile2 = jnp.concatenate([in_tile_b] * 2, axis=1)
     in_tile2v = jnp.concatenate([in_tile_b] * 2, axis=0)
     tile_int = tile_row.astype(jnp.int32)
     window = lax.rem(me_v, HALF_VIEWS) * ROWS + me_c * OWN + tile_int
@@ -315,10 +316,11 @@
     place_x = (lax.rem(window, 32) * TSIDE).astype(F32) + side_at
     place_y = ((window // 32) * TSIDE).astype(F32) + side_at
     acc_ref[...] = jnp.zeros_like(acc_ref)
+    sum_ref[...] = jnp.zeros_like(sum_ref)
 
     pl.semaphore_wait(barrier, VIEWS - 1 + 7)
-    greet_z(near_sem)
-    greet_y(near_sem)
+    signal(near_sem, near_z(1))
+    signal(near_sem, near_z(2))
 
     def table_copy(at):
         to = peers_v[at]
@@ -350,7 +352,7 @@
         for at in arrivals:
             table_wait(at)
         if group == 0:
-            pl.semaphore_wait(near_sem, 7)
+            pl.semaphore_wait(near_sem, 2)
             greet_y(line_sem)
         blocks, highs = [], []
         for step in steps:
@@ -427,7 +429,8 @@
             keep = 1.0 - alpha
             weight = alpha * through
             w_ref[kk, rows, :] = weight
-            rho_ref[kk, rows, :] = alpha / keep
+            inverse = pl.reciprocal(keep, approx=True)
+            rho_ref[kk, rows, :] = alpha * (inverse * (2.0 - keep * inverse))
             for ch in range(3):
                 sums[ch] = sums[ch] + weight * value(kk, 4 + ch)
             through = through * keep
@@ -442,12 +445,12 @@
 
     lax.fori_loop(0, 8, forward, 0)
 
-    prefix = jnp.exp(dot(jnp.concatenate(split3(pre_ref[...]), axis=1), ahead3))
+    prefix = jnp.exp(dot(jnp.concatenate(split2(pre_ref[...]), axis=1), ahead2))
     pre_ref[...] = prefix
     owed = jnp.zeros((PIX, LANES), F32)
     for ch in range(3):
         seen = prefix * part_ref[ch]
-        image = dot(in_tile3, jnp.concatenate(split3(seen), axis=1), ((1,), (1,)))
+        image = dot(in_tile2, jnp.concatenate(split2(seen), axis=1), ((1,), (1,)))
         rend_ref[pl.ds(2 * ch, OWN, stride=6), :] = image[:, :LANES]
         rend_ref[pl.ds(2 * ch + 1, OWN, stride=6), :] = image[:, LANES:]
         miss = image - tgt_ref[ch].astype(F32)
@@ -464,23 +467,21 @@
         pulled = [gl_ref[ch, rows, :] for ch in range(3)]
         for kk in reversed(range(SUB)):
             weight = prefix * w_ref[kk, rows, :]
-            gain = (
-                pulled[0] * value(kk, 4) + pulled[1] * value(kk, 5) + pulled[2] * value(kk, 6)
-            )
-            owed = weight * gain
+            tints = [weight * pulled[ch] for ch in range(3)]
+            owed = tints[0] * value(kk, 4) + tints[1] * value(kk, 5) + tints[2] * value(kk, 6)
             pull = owed - behind * rho_ref[kk, rows, :]
             behind = behind + owed
             up, down = pull[:16], pull[16:]
+            acc_ref[kk] += up + down
             dy_up = dy_ref[kk, pl.ds(2 * i, 1), :]
             dy_down = dy_ref[kk, pl.ds(2 * i + 1, 1), :]
-            acc_ref[kk, 0] += up + down
-            along = up * dy_up
-            along_down = down * dy_down
-            acc_ref[kk, 1] += along + along_down
-            acc_ref[kk, 2] += along * dy_up + along_down * dy_down
+            along_up = (up[:8] + up[8:]) * dy_up
+            along_down = (down[:8] + down[8:]) * dy_down
+            sum_ref[kk, 0] += along_up + along_down
+            sum_ref[kk, 1] += along_up * dy_up + along_down * dy_down
             for ch in range(3):
-                tint = weight * pulled[ch]
-                acc_ref[kk, 3 + ch] += tint[:16] + tint[16:]
+                tint = tints[ch]
+                sum_ref[kk, 2 + ch] += (tint[:8] + tint[8:16]) + (tint[16:24] + tint[24:])
         return carry
 
     lax.fori_loop(0, 8, backward, 0)
@@ -489,20 +490,21 @@
     for kk in range(SUB):
         dx = place_x - value(kk, 0)
         inv = value(kk, 2)
-        base = acc_ref[kk, 0]
+        base = acc_ref[kk]
         base_x = base * dx
+        base_xx = base_x * dx
 
         def total(x):
             return jnp.sum(x, axis=0, keepdims=True)
 
         results += [
             inv * total(base_x),
-            inv * total(acc_ref[kk, 1]),
-            inv * total(base_x * dx + acc_ref[kk, 2]),
+            inv * total(sum_ref[kk, 0]),
+            inv * total((base_xx[:8] + base_xx[8:]) + sum_ref[kk, 1]),
             (1.0 - value(kk, 3)) * total(base),
-            total(acc_ref[kk, 3]),
-            total(acc_ref[kk, 4]),
-            total(acc_ref[kk, 5]),
+            total(sum_ref[kk, 2]),
+            total(sum_ref[kk, 3]),
+            total(sum_ref[kk, 4]),
             jnp.zeros((1, LANES), F32),
         ]
     lists = rows_to_lists(jnp.concatenate(results, axis=0))
@@ -703,7 +705,8 @@
             pltpu.VMEM((PIX, LANES), F32),
             pltpu.VMEM((PIX, LANES), F32),
             pltpu.VMEM((3, PIX, LANES), F32),
-            pltpu.VMEM((SUB, 6, TSIDE, LANES), F32),
+            pltpu.VMEM((SUB, TSIDE, LANES), F32),
+            pltpu.VMEM((SUB, 5, SUB, LANES), F32),
             pltpu.VMEM((2, HIGHS * SUB // 2, SUB * LANES), BF16),
             sems((VIEWS,)),
             sems((VIEWS,)),

time: 37.5 us -> 37.1 us (0.989)
  Pallas kernels: 36.8 us -> 36.4 us
    pallas_call x1, Pallas kernels: 35.6 us -> 35.2 us  [per_device(): pl.pallas_call(step_kernel, out_shape=(jax.ShapeDtypeStruct((96, LANES),...]
where the time goes in v4:
time: 37.1 us; the launch traced here: 37 us
  Pallas kernels  36.4 us (98%)
  between operations  0.64 us (2%)
    pallas_call x1, Pallas kernels, per_device(): pl.pallas_call(step_kernel, out_shape=(jax.ShapeDtypeStruct((96, LANES),...  35.2 us
    pallas_call x1, Pallas kernels, per_device(): pl.pallas_call(adam_kernel, out_shape=(jax.ShapeDtypeStruct((96, LANES),...  1.2 us

profile of v4, /device:TPU:1, one launch (start us, length us, event | category | flops | bytes accessed | tf_op | source)
XLA Modules:
  0.0 37.0 jit_solution(16002741933458002466)
XLA Ops:
  0.6 35.2 %splat_step.1 = (f32[96,128]{1,0:T(8,128)S(1)}, f32[2,8,1024]{2,1,0:T(8,128)S(1)}, f32[2,16,128]{2,1,0:T(8,128)S(1)}, f32[2,2,4]{2,1,0:T(2,128)S(1)}, f32[53,102...) custom-call(f32[53,1024]{1,0:T(8,128)} %g_hbm.1, f32[53,1024]{1,0:T(8,128)} %one_hbm.1, ...), custom_call_target="tpu_custom_call" | custom-call | tf_op jit(solution)/shard_map/splat_step/pallas_call | solution.py:669
  35.9 1.2 %adam.1 = (f32[96,128]{1,0:T(8,128)}, f32[53,1024]{1,0:T(8,128)}, f32[53,1024]{1,0:T(8,128)}, f32[53,1024]{1,0:T(8,128)}) custom-call(f32[2,8,1024]{2,1,0:T(8,128)S(1)} %get-tuple-element.15.grad_ref, f32[96,128]{1,0:T(8,128)S(1)} %get-tuple-element.16.rend_ref, f32[2,16,128]{2,1,0:T(8,128)S(1)} %get-tuple-element.17.basis_ref, ...), custom_call_target="tpu_custom_call" | custom-call | tf_op jit(solution)/shard_map/adam/pallas_call | solution.py:741

commit v5 on v4

--- a/solution.py
+++ b/solution.py
@@ -287,6 +287,87 @@
         for part in range(3):
             oh_ref[part * LANES : (part + 1) * LANES, kk * LANES : (kk + 1) * LANES] = hot
 
+    pl.semaphore_wait(barrier, VIEWS - 1 + 7)
+    signal(near_sem, near_z(1))
+    signal(near_sem, near_z(2))
+
+    def table_copy(at):
+        to = peers_v[at]
+        return pltpu.make_async_remote_copy(
+            src_ref=tab_send.at[to // HALF_VIEWS],
+            dst_ref=tab_recv.at[me_v],
+            send_sem=sem_ts.at[at],
+            recv_sem=sem_tr.at[me_v],
+            device_id=(me_c, to),
+            device_id_type=pl.DeviceIdType.MESH,
+        )
+
+    def table_wait(at):
+        pltpu.make_async_remote_copy(
+            src_ref=tab_send.at[0],
+            dst_ref=tab_recv.at[peers_v[at]],
+            send_sem=sem_ts.at[at],
+            recv_sem=sem_tr.at[peers_v[at]],
+            device_id=(me_c, peers_v[at]),
+            device_id_type=pl.DeviceIdType.MESH,
+        ).wait_recv()
+
+    for at in range(VIEWS - 1):
+        table_copy(at).start()
+    tab_recv[me_v] = tab_send[me_v // HALF_VIEWS]
+
+    chosen = [jnp.zeros((SUB, LANES), F32) for kk in range(SUB)]
+    for group, (steps, arrivals) in enumerate((((0,), (6,)), ((1, 3), (2, 3, 4, 5)), ((2,), (0, 1)))):
+        for at in arrivals:
+            table_wait(at)
+        if group == 0:
+            pl.semaphore_wait(near_sem, 2)
+            greet_y(line_sem)
+        blocks, highs = [], []
+        for step in steps:
+            for core in range(2):
+                home = chip_v(step) + core
+                for at in range(SUB):
+                    blocks.append(tab_recv[home, :, at * LANES : (at + 1) * LANES])
+                    highs.append((home * SUB + at).astype(F32))
+        lhs = jnp.concatenate(split3(jnp.concatenate(blocks, axis=0)), axis=1)
+        for pair in range(4):
+            got = dot(lhs, oh_ref[:, pair * 256 : (pair + 1) * 256])
+            for side in range(2):
+                kk = 2 * pair + side
+                hi = hi_ref[kk : kk + 1, :]
+                for at, value_at in enumerate(highs):
+                    chosen[kk] = chosen[kk] + jnp.where(
+                        hi == value_at,
+                        got[at * SUB : (at + 1) * SUB, side * LANES : (side + 1) * LANES],
+                        0.0,
+                    )
+    lists = rows_to_lists(jnp.concatenate(chosen, axis=0))
+    fwd_send[:, 0, :] = lists[:CELLS]
+    fwd_send[:, 1, :] = lists[CELLS:]
+
+    def cell_copy(source, target, sems, d):
+        return pltpu.make_async_remote_copy(
+            src_ref=source.at[peer_c(d)],
+            dst_ref=target.at[me_c],
+            send_sem=sems.at[0],
+            recv_sem=sems.at[1],
+            device_id=(peer_c(d), me_v),
+            device_id_type=pl.DeviceIdType.MESH,
+        )
+
+    def cell_wait(buffer, sem):
+        others = buffer.at[pl.ds(0, CELLS - 1)]
+        pltpu.make_async_copy(others, others, sem).wait()
+
+    def fwd_start(d, carry):
+        cell_copy(fwd_send, fwd_recv, sem_f, d).start()
+        return carry
+
+    pl.semaphore_wait(line_sem, 3)
+    lax.fori_loop(1, CELLS, fwd_start, 0)
+    fwd_recv[me_c] = fwd_send[me_c]
+
     both = jnp.concatenate([isl_ref[:, 0, :], isl_ref[:, 1, :]], axis=0).astype(F32)
     at_me = jnp.where(iota((LISTS, CELLS), 1) == me_c, both, 0.0)
     tile_half = jnp.sum(at_me, axis=1, keepdims=True)
@@ -318,87 +399,6 @@
     acc_ref[...] = jnp.zeros_like(acc_ref)
     sum_ref[...] = jnp.zeros_like(sum_ref)
 
-    pl.semaphore_wait(barrier, VIEWS - 1 + 7)
-    signal(near_sem, near_z(1))
-    signal(near_sem, near_z(2))
-
-    def table_copy(at):
-        to = peers_v[at]
-        return pltpu.make_async_remote_copy(
-            src_ref=tab_send.at[to // HALF_VIEWS],
-            dst_ref=tab_recv.at[me_v],
-            send_sem=sem_ts.at[at],
-            recv_sem=sem_tr.at[me_v],
-            device_id=(me_c, to),
-            device_id_type=pl.DeviceIdType.MESH,
-        )
-
-    def table_wait(at):
-        pltpu.make_async_remote_copy(
-            src_ref=tab_send.at[0],
-            dst_ref=tab_recv.at[peers_v[at]],
-            send_sem=sem_ts.at[at],
-            recv_sem=sem_tr.at[peers_v[at]],
-            device_id=(me_c, peers_v[at]),
-            device_id_type=pl.DeviceIdType.MESH,
-        ).wait_recv()
-
-    for at in range(VIEWS - 1):
-        table_copy(at).start()
-    tab_recv[me_v] = tab_send[me_v // HALF_VIEWS]
-
-    chosen = [jnp.zeros((SUB, LANES), F32) for kk in range(SUB)]
-    for group, (steps, arrivals) in enumerate((((0,), (6,)), ((1, 3), (2, 3, 4, 5)), ((2,), (0, 1)))):
-        for at in arrivals:
-            table_wait(at)
-        if group == 0:
-            pl.semaphore_wait(near_sem, 2)
-            greet_y(line_sem)
-        blocks, highs = [], []
-        for step in steps:
-            for core in range(2):
-                home = chip_v(step) + core
-                for at in range(SUB):
-                    blocks.append(tab_recv[home, :, at * LANES : (at + 1) * LANES])
-                    highs.append((home * SUB + at).astype(F32))
-        lhs = jnp.concatenate(split3(jnp.concatenate(blocks, axis=0)), axis=1)
-        for pair in range(4):
-            got = dot(lhs, oh_ref[:, pair * 256 : (pair + 1) * 256])
-            for side in range(2):
-                kk = 2 * pair + side
-                hi = hi_ref[kk : kk + 1, :]
-                for at, value_at in enumerate(highs):
-                    chosen[kk] = chosen[kk] + jnp.where(
-                        hi == value_at,
-                        got[at * SUB : (at + 1) * SUB, side * LANES : (side + 1) * LANES],
-                        0.0,
-                    )
-    lists = rows_to_lists(jnp.concatenate(chosen, axis=0))
-    fwd_send[:, 0, :] = lists[:CELLS]
-    fwd_send[:, 1, :] = lists[CELLS:]
-
-    def cell_copy(source, target, sems, d):
-        return pltpu.make_async_remote_copy(
-            src_ref=source.at[peer_c(d)],
-            dst_ref=target.at[me_c],
-            send_sem=sems.at[0],
-            recv_sem=sems.at[1],
-            device_id=(peer_c(d), me_v),
-            device_id_type=pl.DeviceIdType.MESH,
-        )
-
-    def cell_wait(buffer, sem):
-        others = buffer.at[pl.ds(0, CELLS - 1)]
-        pltpu.make_async_copy(others, others, sem).wait()
-
-    def fwd_start(d, carry):
-        cell_copy(fwd_send, fwd_recv, sem_f, d).start()
-        return carry
-
-    pl.semaphore_wait(line_sem, 3)
-    lax.fori_loop(1, CELLS, fwd_start, 0)
-    fwd_recv[me_c] = fwd_send[me_c]
-
     cell_wait(fwd_recv, sem_f.at[1])
     v_ref[...] = lists_to_rows(
         jnp.concatenate([fwd_recv[:, 0, :], fwd_recv[:, 1, :]], axis=0)
@@ -416,15 +416,15 @@
         dy_ref[kk] = dy
 
     def forward(i, carry):
-        rows = pl.ds(pl.multiple_of(i * 32, 32), 32)
-        through = jnp.ones((32, LANES), F32)
-        second = jnp.ones((32, LANES), F32)
+        rows = pl.ds(pl.multiple_of(i * 64, 64), 64)
+        through = jnp.ones((64, LANES), F32)
+        second = jnp.ones((64, LANES), F32)
         first = through
-        sums = [jnp.zeros((32, LANES), F32) for ch in range(3)]
+        sums = [jnp.zeros((64, LANES), F32) for ch in range(3)]
         for kk in range(SUB):
             ex = ex_ref[kk]
             alpha = jnp.concatenate(
-                [ex * ey_ref[kk, pl.ds(2 * i + at, 1), :] for at in range(2)], axis=0
+                [ex * ey_ref[kk, pl.ds(4 * i + at, 1), :] for at in range(4)], axis=0
             )
             keep = 1.0 - alpha
             weight = alpha * through
@@ -443,7 +443,7 @@
         pre_ref[rows, :] = jnp.log(first) + jnp.log(second)
         return carry
 
-    lax.fori_loop(0, 8, forward, 0)
+    lax.fori_loop(0, 4, forward, 0, unroll=True)
 
     prefix = jnp.exp(dot(jnp.concatenate(split2(pre_ref[...]), axis=1), ahead2))
     pre_ref[...] = prefix
@@ -484,7 +484,7 @@
                 sum_ref[kk, 2 + ch] += (tint[:8] + tint[8:16]) + (tint[16:24] + tint[24:])
         return carry
 
-    lax.fori_loop(0, 8, backward, 0)
+    lax.fori_loop(0, 8, backward, 0, unroll=True)
 
     results = []
     for kk in range(SUB):

time: 37.1 us -> 36.4 us (0.981)
  Pallas kernels: 36.4 us -> 35.6 us
    pallas_call x1, Pallas kernels: 35.2 us -> 34.5 us  [per_device(): pl.pallas_call(step_kernel, out_shape=(jax.ShapeDtypeStruct((96, LANES),...]
where the time goes in v5:
time: 36.4 us; the launch traced here: 36.3 us
  Pallas kernels  35.6 us (98%)
  between operations  0.64 us (2%)
    pallas_call x1, Pallas kernels, per_device(): pl.pallas_call(step_kernel, out_shape=(jax.ShapeDtypeStruct((96, LANES),...  34.5 us
    pallas_call x1, Pallas kernels, per_device(): pl.pallas_call(adam_kernel, out_shape=(jax.ShapeDtypeStruct((96, LANES),...  1.2 us

profile of v5, /device:TPU:1, one launch (start us, length us, event | category | flops | bytes accessed | tf_op | source)
XLA Modules:
  0.0 36.3 jit_solution(12942995021111676058)
XLA Ops:
  0.6 34.5 %splat_step.1 = (f32[96,128]{1,0:T(8,128)S(1)}, f32[2,8,1024]{2,1,0:T(8,128)S(1)}, f32[2,16,128]{2,1,0:T(8,128)S(1)}, f32[2,2,4]{2,1,0:T(2,128)S(1)}, f32[53,102...) custom-call(f32[53,1024]{1,0:T(8,128)} %g_hbm.1, f32[53,1024]{1,0:T(8,128)} %one_hbm.1, ...), custom_call_target="tpu_custom_call" | custom-call | tf_op jit(solution)/shard_map/splat_step/pallas_call | solution.py:669
  35.1 1.2 %adam.1 = (f32[96,128]{1,0:T(8,128)}, f32[53,1024]{1,0:T(8,128)}, f32[53,1024]{1,0:T(8,128)}, f32[53,1024]{1,0:T(8,128)}) custom-call(f32[2,8,1024]{2,1,0:T(8,128)S(1)} %get-tuple-element.15.grad_ref, f32[96,128]{1,0:T(8,128)S(1)} %get-tuple-element.16.rend_ref, f32[2,16,128]{2,1,0:T(8,128)S(1)} %get-tuple-element.17.basis_ref, ...), custom_call_target="tpu_custom_call" | custom-call | tf_op jit(solution)/shard_map/adam/pallas_call | solution.py:741

commit v6 on v5

--- a/solution.py
+++ b/solution.py
@@ -145,6 +145,7 @@
     grad_send,
     grad_recv,
     oh_ref,
+    oht_ref,
     hi_ref,
     v_ref,
     ex_ref,
@@ -283,7 +284,9 @@
     high = jnp.where(live, high, -1.0)
     hi_ref[...] = high
     for kk in range(SUB):
-        hot = (iota((LANES, LANES), 0).astype(F32) == low[kk : kk + 1]).astype(F32).astype(BF16)
+        hot = (iota((LANES, LANES), 0).astype(F32) == low[kk : kk + 1]).astype(F32)
+        oht_ref[kk * LANES : (kk + 1) * LANES, :] = hot.T.astype(BF16)
+        hot = hot.astype(BF16)
         for part in range(3):
             oh_ref[part * LANES : (part + 1) * LANES, kk * LANES : (kk + 1) * LANES] = hot
 
@@ -526,7 +529,7 @@
     for kk in range(SUB):
         piece = split2(jnp.where(last, 1.0, grads[kk * SUB : (kk + 1) * SUB]))
         pieces.append([x.astype(F32) for x in piece])
-    hot = oh_ref[0:LANES, :]
+    hot = oht_ref[...]
 
     def grad_copy(at):
         return pltpu.make_async_remote_copy(
@@ -567,8 +570,8 @@
                         ).astype(BF16)
                     )
         rows = slice(0, count * SUB)
-        spread = dot(lhs_ref[0, rows, :], hot, ((1,), (1,)))
-        spread = spread + dot(lhs_ref[1, rows, :], hot, ((1,), (1,)))
+        spread = dot(lhs_ref[0, rows, :], hot)
+        spread = spread + dot(lhs_ref[1, rows, :], hot)
         for which, home in enumerate(homes):
             for at in range(SUB):
                 row = (which * SUB + at) * SUB
@@ -694,6 +697,7 @@
             pltpu.VMEM((VIEWS, SUB, HOME), F32),
             pltpu.VMEM((VIEWS, SUB, HOME), F32),
             pltpu.VMEM((3 * LANES, SUB * LANES), BF16),
+            pltpu.VMEM((SUB * LANES, LANES), BF16),
             pltpu.VMEM((SUB, LANES), F32),
             pltpu.VMEM((64, LANES), F32),
             pltpu.VMEM((SUB, TSIDE, LANES), F32),

time: 36.4 us -> 36.3 us (level)
  no operation moved by 1% of the time
where the time goes in v6:
time: 36.3 us; the launch traced here: 36.2 us
  Pallas kernels  35.6 us (98%)
  between operations  0.64 us (2%)
    pallas_call x1, Pallas kernels, per_device(): pl.pallas_call(step_kernel, out_shape=(jax.ShapeDtypeStruct((96, LANES),...  34.4 us
    pallas_call x1, Pallas kernels, per_device(): pl.pallas_call(adam_kernel, out_shape=(jax.ShapeDtypeStruct((96, LANES),...  1.2 us

profile of v6, /device:TPU:1, one launch (start us, length us, event | category | flops | bytes accessed | tf_op | source)
XLA Modules:
  0.0 36.2 jit_solution(735427153100141826)
XLA Ops:
  0.6 34.4 %splat_step.1 = (f32[96,128]{1,0:T(8,128)S(1)}, f32[2,8,1024]{2,1,0:T(8,128)S(1)}, f32[2,16,128]{2,1,0:T(8,128)S(1)}, f32[2,2,4]{2,1,0:T(2,128)S(1)}, f32[53,102...) custom-call(f32[53,1024]{1,0:T(8,128)} %g_hbm.1, f32[53,1024]{1,0:T(8,128)} %one_hbm.1, ...), custom_call_target="tpu_custom_call" | custom-call | tf_op jit(solution)/shard_map/splat_step/pallas_call | solution.py:672
  35.0 1.2 %adam.1 = (f32[96,128]{1,0:T(8,128)}, f32[53,1024]{1,0:T(8,128)}, f32[53,1024]{1,0:T(8,128)}, f32[53,1024]{1,0:T(8,128)}) custom-call(f32[2,8,1024]{2,1,0:T(8,128)S(1)} %get-tuple-element.15.grad_ref, f32[96,128]{1,0:T(8,128)S(1)} %get-tuple-element.16.rend_ref, f32[2,16,128]{2,1,0:T(8,128)S(1)} %get-tuple-element.17.basis_ref, ...), custom_call_target="tpu_custom_call" | custom-call | tf_op jit(solution)/shard_map/adam/pallas_call | solution.py:745
